TPU v7x, 512 devices: a whole 4x8x8 slice. The times are simulated.
512 devices in a mesh: gx: 64 (over y, x, z_hi), gy: 8 (over z_lo, core).
Axes of the slice: x: 4, y: 8, z: 8 (z_hi: 2, z_lo: 4; z = z_hi * 4 + z_lo), core: 2. Of those that a mesh axis runs over, the one named last changes fastest.
Arguments:
- position: float32 [3, 64, 128, 1024], P(None, None, 'gx', 'gy'), may hold values from 0 to 1
- velocity: float32 [3, 64, 128, 1024], P(None, None, 'gx', 'gy'), may hold values from -4 to 4
- particle_mass: float32 [64, 128, 1024], P(None, 'gx', 'gy'), may hold values from 0.0078125 to 0.03125
- counts: int32 [128, 1024], P('gx', 'gy'), may hold values from 16 to 64
Outputs:
- density: float32 [64, 128, 1024], P(None, 'gx', 'gy')
- acceleration: float32 [3, 64, 128, 1024], P(None, None, 'gx', 'gy')
All inputs are finite; a program needn't handle non-finite values.
Results may differ from a plain program's by a relative error of at most 0.0003.
Values sent between devices are 32-bit elements; how exact they have to be, the bound alone decides.
A program may use at most 64 MiB of HBM per device.

v0:
```python
import jax
import jax.numpy as jnp
from jax import lax
from jax.sharding import PartitionSpec as P

KERNEL_NORM = 21.0 / (2.0 * 3.141592653589793)
REST_DENSITY = 0.5
VISCOSITY = 0.5
SMOOTHING = 0.5
WALL_STIFFNESS = 4.0


def padded(cells, sides, width):
    for axis, dim in sides:
        count = lax.axis_size(axis)
        head = lax.slice_in_dim(cells, 0, width, axis=dim)
        tail = lax.slice_in_dim(cells, cells.shape[dim] - width, cells.shape[dim], axis=dim)
        cells = jnp.concatenate(
            [
                lax.ppermute(tail, axis, [(i, (i + 1) % count) for i in range(count)]),
                cells,
                lax.ppermute(head, axis, [((i + 1) % count, i) for i in range(count)]),
            ],
            axis=dim,
        )
    return cells


def pair_geometry(own_cells, near_cells, shift_x, shift_y):
    sep_x = own_cells[0][:, None] - near_cells[0][None, :] - shift_x
    sep_y = own_cells[1][:, None] - near_cells[1][None, :] - shift_y
    sep_z = own_cells[2][:, None] - near_cells[2][None, :]
    distance_sq = sep_x * sep_x + sep_y * sep_y + sep_z * sep_z
    distance = jnp.sqrt(distance_sq)
    spline = jnp.maximum(1.0 - distance, 0.0)
    return (sep_x, sep_y, sep_z, distance_sq, distance, spline)


def density_kernel(own_cells, near_cells, shift_x, shift_y):
    geometry = pair_geometry(own_cells, near_cells, shift_x, shift_y)
    spline_sq = geometry[5] * geometry[5]
    return KERNEL_NORM * spline_sq * spline_sq * (1.0 + 4.0 * geometry[4])


def density_terms(own_cells, near_cells, shift_x, shift_y):
    kernel = density_kernel(own_cells, near_cells, shift_x, shift_y)
    return jnp.sum(near_cells[6][None, :] * kernel, axis=1)


def pressure_term(density_value):
    return (density_value - REST_DENSITY) / (density_value * density_value)


def force_kernel(own_cells, own_rho, near_cells, near_rho, shift_x, shift_y):
    sep_x, sep_y, sep_z, distance_sq, distance, spline = pair_geometry(
        own_cells, near_cells, shift_x, shift_y
    )
    closing = (
        (own_cells[3][:, None] - near_cells[3][None, :]) * sep_x
        + (own_cells[4][:, None] - near_cells[4][None, :]) * sep_y
        + (own_cells[5][:, None] - near_cells[5][None, :]) * sep_z
    )
    approach = SMOOTHING * jnp.minimum(closing, 0.0) / (distance_sq + 0.01 * SMOOTHING * SMOOTHING)
    mean_rho = 0.5 * (own_rho[:, None] + near_rho[None, :])
    damping = -VISCOSITY * approach / mean_rho
    kernel_slope = -20.0 * KERNEL_NORM * spline * spline * spline
    strength = (
        pressure_term(own_rho)[:, None] + pressure_term(near_rho)[None, :] + damping
    ) * kernel_slope
    return (strength, sep_x, sep_y, sep_z)


def force_terms(own_cells, own_rho, near_cells, near_rho, shift_x, shift_y):
    strength, sep_x, sep_y, sep_z = force_kernel(
        own_cells, own_rho, near_cells, near_rho, shift_x, shift_y
    )
    pair_weight = near_cells[6][None, :] * strength
    return jnp.stack(
        [
            -jnp.sum(pair_weight * sep_x, axis=1),
            -jnp.sum(pair_weight * sep_y, axis=1),
            -jnp.sum(pair_weight * sep_z, axis=1),
        ]
    )


def stencil_density(own_cells, extended):
    width_x = own_cells.shape[2]
    width_y = own_cells.shape[3]
    summed = jnp.zeros(own_cells.shape[1:], jnp.float32)
    for shift_x in (-1, 0, 1):
        for shift_y in (-1, 0, 1):
            near_cells = extended[
                :, :, 1 + shift_x : 1 + shift_x + width_x, 1 + shift_y : 1 + shift_y + width_y
            ]
            summed = summed + density_terms(own_cells, near_cells, float(shift_x), float(shift_y))
    return summed


def stencil_force(own_cells, own_rho, extended, halo_rho):
    width_x = own_cells.shape[2]
    width_y = own_cells.shape[3]
    summed = jnp.zeros((3,) + own_cells.shape[1:], jnp.float32)
    for shift_x in (-1, 0, 1):
        for shift_y in (-1, 0, 1):
            near_cells = extended[
                :, :, 1 + shift_x : 1 + shift_x + width_x, 1 + shift_y : 1 + shift_y + width_y
            ]
            near_rho = halo_rho[
                :, 1 + shift_x : 1 + shift_x + width_x, 1 + shift_y : 1 + shift_y + width_y
            ]
            summed = summed + force_terms(
                own_cells, own_rho, near_cells, near_rho, float(shift_x), float(shift_y)
            )
    return summed


def slot_blocks(per_block, slot_count, slot_group):
    first_slots = jnp.arange(slot_count // slot_group, dtype=jnp.int32) * slot_group
    return lax.map(per_block, first_slots)


def wall_rims(extended, width):
    axis_count = lax.axis_size("gy")
    axis_place = lax.axis_index("gy")
    row_count = extended.shape[3]
    row_index = jnp.arange(row_count, dtype=jnp.int32)
    outside = (row_index < width) & (axis_place == 0) | (row_index >= row_count - width) & (
        axis_place == axis_count - 1
    )
    return jnp.where(outside[None, None, None, :], 0.0, extended)


def on_device(position, velocity, particle_mass, counts):
    slot_count = position.shape[1]
    width_x = counts.shape[0]
    width_y = counts.shape[1]
    slot_group = min(8, slot_count)
    occupied = jnp.arange(slot_count, dtype=jnp.int32)[:, None, None] < counts[None]
    live_mass = jnp.where(occupied, particle_mass, 0.0)
    fields = jnp.concatenate([position, velocity, live_mass[None]], axis=0)
    extended = wall_rims(padded(fields, (("gx", 2), ("gy", 3)), 1), 1)

    def density_block(first_slot):
        return stencil_density(
            lax.dynamic_slice_in_dim(fields, first_slot, slot_group, 1), extended
        )

    blocks = slot_blocks(density_block, slot_count, slot_group)
    rho_raw = blocks.reshape((slot_count,) + blocks.shape[2:])
    rho_safe = jnp.where(occupied, rho_raw, 1.0)
    halo_rho = padded(rho_safe, (("gx", 1), ("gy", 2)), 1)
    halo_rho = jnp.where(extended[6] > 0.0, halo_rho, 1.0)

    def force_block(first_slot):
        own_cells = lax.dynamic_slice_in_dim(fields, first_slot, slot_group, 1)
        own_rho = lax.dynamic_slice_in_dim(rho_safe, first_slot, slot_group, 0)
        return stencil_force(own_cells, own_rho, extended, halo_rho)

    blocks = slot_blocks(force_block, slot_count, slot_group)
    acceleration = jnp.transpose(blocks, (1, 0, 2, 3, 4)).reshape((3, slot_count, width_x, width_y))
    rows_first = lax.axis_index("gy") * width_y
    height = (rows_first + jnp.arange(width_y, dtype=jnp.int32)).astype(jnp.float32)[
        None, None, :
    ] + position[1]
    channel = float(width_y * lax.axis_size("gy"))
    near_floor = jnp.maximum(1.0 - 2.0 * height, 0.0)
    near_ceiling = jnp.maximum(1.0 - 2.0 * (channel - height), 0.0)
    wall_push = WALL_STIFFNESS * (near_floor * near_floor - near_ceiling * near_ceiling)
    acceleration = jnp.stack([acceleration[0], acceleration[1] + wall_push, acceleration[2]])
    density = jnp.where(occupied, rho_raw, 0.0)
    acceleration = jnp.where(occupied[None], acceleration, 0.0)
    return (density, acceleration)


def solution(mesh):
    in_specs = (
        P(None, None, "gx", "gy"),
        P(None, None, "gx", "gy"),
        P(None, "gx", "gy"),
        P("gx", "gy"),
    )
    out_specs = (P(None, "gx", "gy"), P(None, None, "gx", "gy"))
    return jax.shard_map(
        on_device, mesh=mesh, in_specs=in_specs, out_specs=out_specs, check_vma=False
    )
```

profile of v0, /device:TPU:1, one launch (start us, length us, event | category | flops | bytes accessed | tf_op | source)
XLA Modules:
  0.0 256.3 jit_solution(12069955917739939313)
XLA Ops:
  3.5 11.5 %collective-permute-start = (f32[7,64,1,128]{3,1,2,0:T(8,128)S(1)}, f32[7,64,1,128]{3,1,2,0:T(8,128)S(1)}, u32[]{:S(2)}, u32[]{:S(2)}) collective-permute-start(f32[7,64,1,128]{3,1,2,0:T(8,128)S(1)} %get-tuple-element.620), channel_id=1, source_target_pairs={{0,8},{8,16},{16,24},{24,32},{32,40},{40,48},{48,56},{56,64},{64,7... | collective-permute-start | bytes 688136 | tf_op jit(solution)/shard_map/ppermute | solution.py:20
  14.9 7.0 %collective-permute-start.1 = (f32[7,64,1,128]{3,1,2,0:T(8,128)S(1)}, f32[7,64,1,128]{3,1,2,0:T(8,128)S(1)}, u32[]{:S(2)}, u32[]{:S(2)}) collective-permute-start(f32[7,64,1,128]{3,1,2,0:T(8,128)S(1)} %get-tuple-element.621), channel_id=1, source_target_pairs={{8,0},{16,8},{24,16},{32,24},{40,32},{48,40},{56,48},{64,56},{72,6... | collective-permute-start | bytes 688136 | tf_op jit(solution)/shard_map/ppermute | solution.py:22
  22.0 4.5 %collective-permute-done = f32[7,64,1,128]{3,1,2,0:T(8,128)S(1)} collective-permute-done((f32[7,64,1,128]{3,1,2,0:T(8,128)S(1)}, f32[7,64,1,128]{3,1,2,0:T(8,128)S(1)}, u32[]{:S(2)}, u32[]{:S(2)}) %collective-permute-start) | collective-permute-done | bytes 229408 | tf_op jit(solution)/shard_map/ppermute | solution.py:20
  29.6 11.6 %collective-permute-start.2 = (f32[7,64,4,1]{1,2,3,0:T(4,128)S(1)}, f32[7,64,4,1]{1,2,3,0:T(4,128)S(1)}, u32[]{:S(2)}, u32[]{:S(2)}) collective-permute-start(f32[7,64,4,1]{1,2,3,0:T(4,128)S(1)} %copy.56), channel_id=1, source_target_pairs={{0,1},{1,2},{2,3},{3,4},{4,5},{5,6},{6,7},{7,0},{8,9},{9,10},{10,1... | collective-permute-start | bytes 21512 | tf_op jit(solution)/shard_map/ppermute | solution.py:20
  41.6 1.9 collective-permute-start.3
  48.0 2.0 maximum_select_fusion
  50.0 64.9 %while.26 = (s32[]{:T(128)}, f32[8,8,2,128]{3,1,0,2:T(8,128)S(1)}, f32[7,64,4,130]{3,1,2,0:T(8,128)S(1)}, s32[8]{0:T(128)S(1)}, f32[7,64,2,128]{3,2,1,0:T(2,128)...) while((s32[]{:T(128)}, f32[8,8,2,128]{3,1,0,2:T(8,128)S(1)}, f32[7,64,4,130]{3,1,2,0:T(8,128)S(1)}, ...), condition=%wide.region_10.11_spmd, body=%wide.region_0.10_spmd.sunk | while | flops 22804488 | bytes 7372987 | solution.py:120
  55.6 1.9 fusion.158
  63.8 1.9 fusion.158
  114.9 7.6 %collective-permute-start.4 = (f32[64,1,128]{2,0,1:T(8,128)S(1)}, f32[64,1,128]{2,0,1:T(8,128)S(1)}, u32[]{:S(2)}, u32[]{:S(2)}) collective-permute-start(f32[64,1,128]{2,0,1:T(8,128)S(1)} %get-tuple-element.638), channel_id=1, source_target_pairs={{0,8},{8,16},{16,24},{24,32},{32,40},{40,48},{48,56},{56,64},{64,7... | collective-permute-start | bytes 98312 | tf_op jit(solution)/shard_map/ppermute | solution.py:20
  122.5 5.8 %collective-permute-start.5 = (f32[64,1,128]{2,0,1:T(8,128)S(1)}, f32[64,1,128]{2,0,1:T(8,128)S(1)}, u32[]{:S(2)}, u32[]{:S(2)}) collective-permute-start(f32[64,1,128]{2,0,1:T(8,128)S(1)} %get-tuple-element.639), channel_id=1, source_target_pairs={{8,0},{16,8},{24,16},{32,24},{40,32},{48,40},{56,48},{64,56},{72,6... | collective-permute-start | bytes 98312 | tf_op jit(solution)/shard_map/ppermute | solution.py:22
  128.3 2.8 %collective-permute-done.5 = f32[64,1,128]{2,0,1:T(8,128)S(1)} collective-permute-done((f32[64,1,128]{2,0,1:T(8,128)S(1)}, f32[64,1,128]{2,0,1:T(8,128)S(1)}, u32[]{:S(2)}, u32[]{:S(2)}) %collective-permute-start.5) | collective-permute-done | bytes 32800 | tf_op jit(solution)/shard_map/ppermute | solution.py:22
  131.3 4.0 %collective-permute-start.6 = (f32[64,4,1]{2,0,1:T(8,128)S(1)}, f32[64,4,1]{2,0,1:T(8,128)S(1)}, u32[]{:S(2)}, u32[]{:S(2)}) collective-permute-start(f32[64,4,1]{2,0,1:T(8,128)S(1)} %get-tuple-element.634), channel_id=1, source_target_pairs={{0,1},{1,2},{2,3},{3,4},{4,5},{5,6},{6,7},{7,0},{8,9},{9,10},{10,1... | collective-permute-start | bytes 3080 | tf_op jit(solution)/shard_map/ppermute | solution.py:20
  135.3 2.5 collective-permute-start.7
  138.5 4.0 %collective-permute-done.7 = f32[64,4,1]{2,0,1:T(8,128)S(1)} collective-permute-done((f32[64,4,1]{2,0,1:T(8,128)S(1)}, f32[64,4,1]{2,0,1:T(8,128)S(1)}, u32[]{:S(2)}, u32[]{:S(2)}) %collective-permute-start.7) | collective-permute-done | bytes 1056 | tf_op jit(solution)/shard_map/ppermute | solution.py:22
  142.9 111.6 %while.27 = (s32[]{:T(128)}, f32[8,3,8,2,128]{4,3,2,1,0:T(2,128)S(1)}, f32[7,64,4,130]{3,1,2,0:T(8,128)S(1)}, s32[8]{0:T(128)S(1)}, f32[64,2,128]{2,0,1:T(8,128)...) while((s32[]{:T(128)}, ...), condition=%wide.region_39.40_spmd, body=%wide.region_11.39_spmd.sunk | while | flops 48039944 | bytes 17695072 | solution.py:120
  147.5 3.9 %multiply_reduce_fusion.15 = (f32[8,2,128]{2,1,0:T(2,128)S(1)}, f32[8,2,128]{2,1,0:T(2,128)S(1)}, f32[8,2,128]{2,1,0:T(2,128)S(1)}, f32[8,2,128]{2,1,0:T(2,128)S...) fusion(f32[64,2,128]{2,0,1:T(8,128)S(1)} %get-tuple-element.100, ...), kind=kLoop, calls=%fused_computation.245.clone.1 | loop fusion | flops 21209088 | bytes 2523136 | tf_op jit(solution)/shard_map/while/body/eval_jaxpr/reduce_sum | solution.py:80
  151.8 3.8 %multiply_reduce_fusion.16 = (f32[8,2,128]{2,1,0:T(2,128)S(1)}, f32[8,2,128]{2,1,0:T(2,128)S(1)}, f32[8,2,128]{2,1,0:T(2,128)S(1)}, f32[8,2,128]{2,1,0:T(2,128)S...) fusion(f32[64,2,128]{2,0,1:T(8,128)S(1)} %get-tuple-element.105, ...), kind=kLoop, calls=%fused_computation.242.clone.1 | loop fusion | flops 20946944 | bytes 2523136 | tf_op jit(solution)/shard_map/while/body/eval_jaxpr/reduce_sum | solution.py:80
  161.4 3.9 %multiply_reduce_fusion.15 = (f32[8,2,128]{2,1,0:T(2,128)S(1)}, f32[8,2,128]{2,1,0:T(2,128)S(1)}, f32[8,2,128]{2,1,0:T(2,128)S(1)}, f32[8,2,128]{2,1,0:T(2,128)S...) fusion(f32[64,2,128]{2,0,1:T(8,128)S(1)} %get-tuple-element.100, ...), kind=kLoop, calls=%fused_computation.245.clone.1 | loop fusion | flops 21209088 | bytes 2523136 | tf_op jit(solution)/shard_map/while/body/eval_jaxpr/reduce_sum | solution.py:80
  165.7 3.8 %multiply_reduce_fusion.16 = (f32[8,2,128]{2,1,0:T(2,128)S(1)}, f32[8,2,128]{2,1,0:T(2,128)S(1)}, f32[8,2,128]{2,1,0:T(2,128)S(1)}, f32[8,2,128]{2,1,0:T(2,128)S...) fusion(f32[64,2,128]{2,0,1:T(8,128)S(1)} %get-tuple-element.105, ...), kind=kLoop, calls=%fused_computation.242.clone.1 | loop fusion | flops 20946944 | bytes 2523136 | tf_op jit(solution)/shard_map/while/body/eval_jaxpr/reduce_sum | solution.py:80
  175.4 3.9 %multiply_reduce_fusion.15 = (f32[8,2,128]{2,1,0:T(2,128)S(1)}, f32[8,2,128]{2,1,0:T(2,128)S(1)}, f32[8,2,128]{2,1,0:T(2,128)S(1)}, f32[8,2,128]{2,1,0:T(2,128)S...) fusion(f32[64,2,128]{2,0,1:T(8,128)S(1)} %get-tuple-element.100, ...), kind=kLoop, calls=%fused_computation.245.clone.1 | loop fusion | flops 21209088 | bytes 2523136 | tf_op jit(solution)/shard_map/while/body/eval_jaxpr/reduce_sum | solution.py:80
  179.7 3.8 %multiply_reduce_fusion.16 = (f32[8,2,128]{2,1,0:T(2,128)S(1)}, f32[8,2,128]{2,1,0:T(2,128)S(1)}, f32[8,2,128]{2,1,0:T(2,128)S(1)}, f32[8,2,128]{2,1,0:T(2,128)S...) fusion(f32[64,2,128]{2,0,1:T(8,128)S(1)} %get-tuple-element.105, ...), kind=kLoop, calls=%fused_computation.242.clone.1 | loop fusion | flops 20946944 | bytes 2523136 | tf_op jit(solution)/shard_map/while/body/eval_jaxpr/reduce_sum | solution.py:80
  189.3 3.9 %multiply_reduce_fusion.15 = (f32[8,2,128]{2,1,0:T(2,128)S(1)}, f32[8,2,128]{2,1,0:T(2,128)S(1)}, f32[8,2,128]{2,1,0:T(2,128)S(1)}, f32[8,2,128]{2,1,0:T(2,128)S...) fusion(f32[64,2,128]{2,0,1:T(8,128)S(1)} %get-tuple-element.100, ...), kind=kLoop, calls=%fused_computation.245.clone.1 | loop fusion | flops 21209088 | bytes 2523136 | tf_op jit(solution)/shard_map/while/body/eval_jaxpr/reduce_sum | solution.py:80
  193.6 3.8 %multiply_reduce_fusion.16 = (f32[8,2,128]{2,1,0:T(2,128)S(1)}, f32[8,2,128]{2,1,0:T(2,128)S(1)}, f32[8,2,128]{2,1,0:T(2,128)S(1)}, f32[8,2,128]{2,1,0:T(2,128)S...) fusion(f32[64,2,128]{2,0,1:T(8,128)S(1)} %get-tuple-element.105, ...), kind=kLoop, calls=%fused_computation.242.clone.1 | loop fusion | flops 20946944 | bytes 2523136 | tf_op jit(solution)/shard_map/while/body/eval_jaxpr/reduce_sum | solution.py:80
  203.3 3.9 %multiply_reduce_fusion.15 = (f32[8,2,128]{2,1,0:T(2,128)S(1)}, f32[8,2,128]{2,1,0:T(2,128)S(1)}, f32[8,2,128]{2,1,0:T(2,128)S(1)}, f32[8,2,128]{2,1,0:T(2,128)S...) fusion(f32[64,2,128]{2,0,1:T(8,128)S(1)} %get-tuple-element.100, ...), kind=kLoop, calls=%fused_computation.245.clone.1 | loop fusion | flops 21209088 | bytes 2523136 | tf_op jit(solution)/shard_map/while/body/eval_jaxpr/reduce_sum | solution.py:80
  207.6 3.8 %multiply_reduce_fusion.16 = (f32[8,2,128]{2,1,0:T(2,128)S(1)}, f32[8,2,128]{2,1,0:T(2,128)S(1)}, f32[8,2,128]{2,1,0:T(2,128)S(1)}, f32[8,2,128]{2,1,0:T(2,128)S...) fusion(f32[64,2,128]{2,0,1:T(8,128)S(1)} %get-tuple-element.105, ...), kind=kLoop, calls=%fused_computation.242.clone.1 | loop fusion | flops 20946944 | bytes 2523136 | tf_op jit(solution)/shard_map/while/body/eval_jaxpr/reduce_sum | solution.py:80
  217.2 3.9 %multiply_reduce_fusion.15 = (f32[8,2,128]{2,1,0:T(2,128)S(1)}, f32[8,2,128]{2,1,0:T(2,128)S(1)}, f32[8,2,128]{2,1,0:T(2,128)S(1)}, f32[8,2,128]{2,1,0:T(2,128)S...) fusion(f32[64,2,128]{2,0,1:T(8,128)S(1)} %get-tuple-element.100, ...), kind=kLoop, calls=%fused_computation.245.clone.1 | loop fusion | flops 21209088 | bytes 2523136 | tf_op jit(solution)/shard_map/while/body/eval_jaxpr/reduce_sum | solution.py:80
  221.5 3.8 %multiply_reduce_fusion.16 = (f32[8,2,128]{2,1,0:T(2,128)S(1)}, f32[8,2,128]{2,1,0:T(2,128)S(1)}, f32[8,2,128]{2,1,0:T(2,128)S(1)}, f32[8,2,128]{2,1,0:T(2,128)S...) fusion(f32[64,2,128]{2,0,1:T(8,128)S(1)} %get-tuple-element.105, ...), kind=kLoop, calls=%fused_computation.242.clone.1 | loop fusion | flops 20946944 | bytes 2523136 | tf_op jit(solution)/shard_map/while/body/eval_jaxpr/reduce_sum | solution.py:80
  231.2 3.9 %multiply_reduce_fusion.15 = (f32[8,2,128]{2,1,0:T(2,128)S(1)}, f32[8,2,128]{2,1,0:T(2,128)S(1)}, f32[8,2,128]{2,1,0:T(2,128)S(1)}, f32[8,2,128]{2,1,0:T(2,128)S...) fusion(f32[64,2,128]{2,0,1:T(8,128)S(1)} %get-tuple-element.100, ...), kind=kLoop, calls=%fused_computation.245.clone.1 | loop fusion | flops 21209088 | bytes 2523136 | tf_op jit(solution)/shard_map/while/body/eval_jaxpr/reduce_sum | solution.py:80
  235.4 3.8 %multiply_reduce_fusion.16 = (f32[8,2,128]{2,1,0:T(2,128)S(1)}, f32[8,2,128]{2,1,0:T(2,128)S(1)}, f32[8,2,128]{2,1,0:T(2,128)S(1)}, f32[8,2,128]{2,1,0:T(2,128)S...) fusion(f32[64,2,128]{2,0,1:T(8,128)S(1)} %get-tuple-element.105, ...), kind=kLoop, calls=%fused_computation.242.clone.1 | loop fusion | flops 20946944 | bytes 2523136 | tf_op jit(solution)/shard_map/while/body/eval_jaxpr/reduce_sum | solution.py:80
  245.1 3.9 %multiply_reduce_fusion.15 = (f32[8,2,128]{2,1,0:T(2,128)S(1)}, f32[8,2,128]{2,1,0:T(2,128)S(1)}, f32[8,2,128]{2,1,0:T(2,128)S(1)}, f32[8,2,128]{2,1,0:T(2,128)S...) fusion(f32[64,2,128]{2,0,1:T(8,128)S(1)} %get-tuple-element.100, ...), kind=kLoop, calls=%fused_computation.245.clone.1 | loop fusion | flops 21209088 | bytes 2523136 | tf_op jit(solution)/shard_map/while/body/eval_jaxpr/reduce_sum | solution.py:80
  249.4 3.8 %multiply_reduce_fusion.16 = (f32[8,2,128]{2,1,0:T(2,128)S(1)}, f32[8,2,128]{2,1,0:T(2,128)S(1)}, f32[8,2,128]{2,1,0:T(2,128)S(1)}, f32[8,2,128]{2,1,0:T(2,128)S...) fusion(f32[64,2,128]{2,0,1:T(8,128)S(1)} %get-tuple-element.105, ...), kind=kLoop, calls=%fused_computation.242.clone.1 | loop fusion | flops 20946944 | bytes 2523136 | tf_op jit(solution)/shard_map/while/body/eval_jaxpr/reduce_sum | solution.py:80
  (316 shorter events, 90.8 us)
Async XLA Ops:
  3.5 23.0 %collective-permute-start = (f32[7,64,1,128]{3,1,2,0:T(8,128)S(1)}, f32[7,64,1,128]{3,1,2,0:T(8,128)S(1)}, u32[]{:S(2)}, u32[]{:S(2)}) collective-permute-start(f32[7,64,1,128]{3,1,2,0:T(8,128)S(1)} %get-tuple-element.620), channel_id=1, source_target_pairs={{0,8},{8,16},{16,24},{24,32},{32,40},{40,48},{48,56},{56,64},{64,7... | collective-permute-start | bytes 688136 | tf_op jit(solution)/shard_map/ppermute | solution.py:20
  14.9 13.3 %collective-permute-start.1 = (f32[7,64,1,128]{3,1,2,0:T(8,128)S(1)}, f32[7,64,1,128]{3,1,2,0:T(8,128)S(1)}, u32[]{:S(2)}, u32[]{:S(2)}) collective-permute-start(f32[7,64,1,128]{3,1,2,0:T(8,128)S(1)} %get-tuple-element.621), channel_id=1, source_target_pairs={{8,0},{16,8},{24,16},{32,24},{40,32},{48,40},{56,48},{64,56},{72,6... | collective-permute-start | bytes 688136 | tf_op jit(solution)/shard_map/ppermute | solution.py:22
  28.2 0.7 copy-start
  29.6 15.1 %collective-permute-start.2 = (f32[7,64,4,1]{1,2,3,0:T(4,128)S(1)}, f32[7,64,4,1]{1,2,3,0:T(4,128)S(1)}, u32[]{:S(2)}, u32[]{:S(2)}) collective-permute-start(f32[7,64,4,1]{1,2,3,0:T(4,128)S(1)} %copy.56), channel_id=1, source_target_pairs={{0,1},{1,2},{2,3},{3,4},{4,5},{5,6},{6,7},{7,0},{8,9},{9,10},{10,1... | collective-permute-start | bytes 21512 | tf_op jit(solution)/shard_map/ppermute | solution.py:20
  41.6 5.0 %collective-permute-start.3 = (f32[7,64,4,1]{1,2,3,0:T(4,128)S(1)}, f32[7,64,4,1]{1,2,3,0:T(4,128)S(1)}, u32[]{:S(2)}, u32[]{:S(2)}) collective-permute-start(f32[7,64,4,1]{1,2,3,0:T(4,128)S(1)} %copy.57), channel_id=1, source_target_pairs={{1,0},{2,1},{3,2},{4,3},{5,4},{6,5},{7,6},{0,7},{9,8},{10,9},{11,1... | collective-permute-start | bytes 21512 | tf_op jit(solution)/shard_map/ppermute | solution.py:22
  49.9 64.9 %copy-start.1 = (s32[2,128]{1,0:T(2,128)S(1)}, s32[2,128]{1,0:T(2,128)}, u32[]{:S(2)}) copy-start(s32[2,128]{1,0:T(2,128)} %param.11) | copy-start | bytes 3076
  114.9 13.4 %collective-permute-start.4 = (f32[64,1,128]{2,0,1:T(8,128)S(1)}, f32[64,1,128]{2,0,1:T(8,128)S(1)}, u32[]{:S(2)}, u32[]{:S(2)}) collective-permute-start(f32[64,1,128]{2,0,1:T(8,128)S(1)} %get-tuple-element.638), channel_id=1, source_target_pairs={{0,8},{8,16},{16,24},{24,32},{32,40},{40,48},{48,56},{56,64},{64,7... | collective-permute-start | bytes 98312 | tf_op jit(solution)/shard_map/ppermute | solution.py:20
  122.5 8.7 %collective-permute-start.5 = (f32[64,1,128]{2,0,1:T(8,128)S(1)}, f32[64,1,128]{2,0,1:T(8,128)S(1)}, u32[]{:S(2)}, u32[]{:S(2)}) collective-permute-start(f32[64,1,128]{2,0,1:T(8,128)S(1)} %get-tuple-element.639), channel_id=1, source_target_pairs={{8,0},{16,8},{24,16},{32,24},{40,32},{48,40},{56,48},{64,56},{72,6... | collective-permute-start | bytes 98312 | tf_op jit(solution)/shard_map/ppermute | solution.py:22
  131.3 7.3 %collective-permute-start.6 = (f32[64,4,1]{2,0,1:T(8,128)S(1)}, f32[64,4,1]{2,0,1:T(8,128)S(1)}, u32[]{:S(2)}, u32[]{:S(2)}) collective-permute-start(f32[64,4,1]{2,0,1:T(8,128)S(1)} %get-tuple-element.634), channel_id=1, source_target_pairs={{0,1},{1,2},{2,3},{3,4},{4,5},{5,6},{6,7},{7,0},{8,9},{9,10},{10,1... | collective-permute-start | bytes 3080 | tf_op jit(solution)/shard_map/ppermute | solution.py:20
  135.3 7.3 %collective-permute-start.7 = (f32[64,4,1]{2,0,1:T(8,128)S(1)}, f32[64,4,1]{2,0,1:T(8,128)S(1)}, u32[]{:S(2)}, u32[]{:S(2)}) collective-permute-start(f32[64,4,1]{2,0,1:T(8,128)S(1)} %get-tuple-element.635), channel_id=1, source_target_pairs={{1,0},{2,1},{3,2},{4,3},{5,4},{6,5},{7,6},{0,7},{9,8},{10,9},{11,1... | collective-permute-start | bytes 3080 | tf_op jit(solution)/shard_map/ppermute | solution.py:22
where the time goes:
time: 259 us; the launch traced here: 256 us
  other arithmetic  112 us (43%)
  starting transfers between devices  52 us (20%)
  local copies, waits for them, and re-layouts  42.9 us (17%)
  loops' own time  33.9 us (13%)
  waiting for transfers between devices  14.7 us (6%)
    reduce_sum x24, other arithmetic, force_terms(): jnp.sum(pair_weight * sep_x, axis=1)  69.4 us
    ppermute x4, starting transfers between devices, padded(): lax.ppermute(tail, axis, [(i, (i + 1) % count) for i in range(count)])  34.7 us
    another operation x2, loops' own time, slot_blocks(): return lax.map(per_block, first_slots)  33.9 us
    reduce_sum x24, other arithmetic, density_terms(): return jnp.sum(near_cells[6][None, :] * kernel, axis=1)  33.8 us
    ppermute x4, starting transfers between devices, padded(): lax.ppermute(head, axis, [((i + 1) % count, i) for i in range(count)])  17.2 us
    ppermute x4, waiting for transfers between devices, padded(): lax.ppermute(head, axis, [((i + 1) % count, i) for i in range(count)])  10.1 us
    dynamic_slice x16, local copies, waits for them, and re-layouts, slot_blocks(): return lax.map(per_block, first_slots)  10 us
    sub x16, local copies, waits for them, and re-layouts, force_kernel(): own_cells[3][:, None] - near_cells[3][None, :]  8.85 us
  transfers between devices with their start and end apart: 8, of which 5 were waited for; matrix products, arithmetic and copies ran while one was open for 1% of the time, Pallas kernels for 0%

commit v1 on v0

v1 whole, which is shorter than its diff:
```python
import functools

import jax
import jax.numpy as jnp
from jax import lax
from jax.experimental import pallas as pl
from jax.experimental.pallas import tpu as pltpu
from jax.sharding import PartitionSpec as P

MESH = pl.DeviceIdType.MESH
F32 = jnp.float32
KERNEL_NORM = 21.0 / (2.0 * 3.141592653589793)
REST_DENSITY = 0.5
VISCOSITY = 0.5
SMOOTHING = 0.5
WALL_STIFFNESS = 4.0
TINY = 1e-30
SLOTS = 64
LANES = 128

INNER = ((1, 1, 1, 0), (2, 2, 1, 1), (1, 2, 1, 1), (1, 2, 0, 2), (1, 2, -1, 3))
OTHERS = ((0, 1), (1, 1), (1, 0), (1, -1))
UNITS = len(INNER) + 2 + 6


def pressure_term(rho):
    return (rho - REST_DENSITY) / (rho * rho)


def spline_of(dx, dy, dz):
    dist_sq = jnp.maximum(dx * dx + dy * dy + dz * dz, TINY)
    dist = dist_sq * lax.rsqrt(dist_sq)
    return dist, jnp.maximum(1.0 - dist, 0.0)


def density_pair(dist, spline):
    spline_sq = spline * spline
    return spline_sq * spline_sq * (dist + 0.25)


def lane_ids(rows):
    return lax.broadcasted_iota(jnp.int32, (rows, LANES), 1)


def shifted(cells, shift):
    return cells if shift == 0 else pltpu.roll(cells, (-shift) % LANES, 1)


def wrapped_lane(shift):
    return LANES - 1 if shift > 0 else 0


def kernel(
    gx_count, gy_count,
    pos_ref, vel_ref, mass_ref, counts_ref, rho_out, acc_out,
    near_p, near_v, near_r, got_p, got_v, got_r, edge_own, edge_got, edge_rho, edge_rho_got,
    kept, rho_sum, rho_other, force_sum, force_one, force_other, send_sem, recv_sem,
):
    gx = lax.axis_index("gx")
    gy = lax.axis_index("gy")

    def place(step_x, step_y):
        return (lax.rem(gx + step_x + gx_count, gx_count), lax.rem(gy + step_y + gy_count, gy_count))

    barrier = pltpu.get_barrier_semaphore()
    for step_x in (-1, 0, 1):
        for step_y in (-1, 0, 1):
            if step_x != 0 or step_y != 0:
                pl.semaphore_signal(barrier, inc=1, device_id=place(step_x, step_y), device_id_type=MESH)

    for col in range(2):
        rows = pl.ds(col, SLOTS, stride=2)
        slot = lax.broadcasted_iota(jnp.int32, (SLOTS, LANES), 0)
        occupied = slot < counts_ref[col : col + 1, :]
        near_p[1 + col, 1, 0] = pos_ref[0, rows, :] + float(col)
        near_p[1 + col, 1, 1] = pos_ref[1, rows, :]
        near_p[1 + col, 1, 2] = pos_ref[2, rows, :]
        near_p[1 + col, 1, 3] = jnp.where(occupied, mass_ref[rows, :], 0.0)

    pl.semaphore_wait(barrier, 8)

    copies = []

    def send(index, source, target, step_x, step_y):
        copy = pltpu.make_async_remote_copy(
            src_ref=source, dst_ref=target, send_sem=send_sem.at[index], recv_sem=recv_sem.at[index],
            device_id=place(step_x, step_y), device_id_type=MESH,
        )
        copy.start()
        copies.append(copy)
        return copy

    pos_copies = [
        send(0, near_p.at[1, 1], got_p.at[1], -1, 0),
        send(1, near_p.at[2, 1], got_p.at[0], 1, 0),
    ]

    for col in range(2):
        rows = pl.ds(col, SLOTS, stride=2)
        for axis in range(3):
            near_v[1 + col, 1, axis] = SMOOTHING * vel_ref[axis, rows, :]

    def edge_pack(fields, lane):
        ids = lane_ids(SLOTS)
        halves = []
        for col in range(2):
            pack = jnp.zeros((SLOTS, LANES), F32)
            for index, field in enumerate(fields[col]):
                pack = jnp.where(ids == index, field[:, lane : lane + 1], pack)
            halves.append(pack)
        return jnp.concatenate(halves, axis=0).T[0:8, :]

    own_fields = [
        [near_p[1 + col, 1, f] for f in range(4)] + [near_v[1 + col, 1, f] for f in range(3)] for col in range(2)
    ]
    for edge, lane in ((0, 0), (1, LANES - 1)):
        edge_own[edge] = edge_pack(own_fields, lane)
    edge_copies = []
    for edge, step_y in ((0, -1), (1, 1)):
        for which, step_x in enumerate((0, 1, -1)):
            edge_copies.append(
                send(2 + edge * 3 + which, edge_own.at[edge], edge_got.at[1 - edge, which], step_x, step_y)
            )
    vel_copies = [
        send(8, near_v.at[1, 1], got_v.at[1], -1, 0),
        send(9, near_v.at[2, 1], got_v.at[0], 1, 0),
    ]

    def shift_positions(column, columns, first):
        for shift in (-1, 0, 1):
            if first and shift == 0:
                continue
            ids = lane_ids(SLOTS)
            near_p[column, 1 + shift, 0] = shifted(columns[0], shift)
            near_p[column, 1 + shift, 1] = shifted(columns[1], shift) + float(shift)
            near_p[column, 1 + shift, 2] = shifted(columns[2], shift)
            mass = shifted(columns[3], shift)
            if shift != 0:
                mass = jnp.where(ids == wrapped_lane(shift), 0.0, mass)
            near_p[column, 1 + shift, 3] = mass

    for column in (1, 2):
        shift_positions(column, [near_p[column, 1, f] for f in range(4)], True)

    def density_unit(unit, own, near, near_shift, other, fresh):
        for half in range(2):
            rows = slice(32 * half, 32 * half + 32)
            own_x, own_y, own_z, own_m = (near_p[own, 1, f, rows, :] for f in range(4))

            def step(j, total):
                near_x, near_y, near_z, near_m = (near_p[near, near_shift, f, pl.ds(j, 1), :] for f in range(4))
                dist, spline = spline_of(own_x - near_x, own_y - near_y, own_z - near_z)
                kept[unit, j, rows, :] = spline
                pair = density_pair(dist, spline)
                if other is not None:
                    back = (pair * own_m).reshape(4, 8, LANES).sum(axis=0)
                    if half == 0 and fresh:
                        rho_other[other, j] = back
                    else:
                        rho_other[other, j] += back
                return total + pair * near_m

            total = lax.fori_loop(0, SLOTS, step, jnp.zeros((32, LANES), F32), unroll=2)
            rho_sum[own - 1, rows, :] += total

    rho_sum[...] = jnp.zeros_like(rho_sum)
    seen = set()
    for unit, (own, near, shift, other) in enumerate(INNER):
        density_unit(unit, own, near, 1 + shift, other, other not in seen)
        seen.add(other)

    def self_density(col, carry):
        density_unit(len(INNER) + col, 1 + col, 1 + col, 1, None, True)
        return carry

    lax.fori_loop(0, 2, self_density, 0)

    for copy in pos_copies:
        copy.wait()
    for side, move in ((0, -2.0), (1, 2.0)):
        shift_positions(3 * side, [got_p[side, 0] + move] + [got_p[side, f] for f in range(1, 4)], False)

    def outer_density(index, carry):
        side = index // 3
        density_unit(len(INNER) + 2 + index, 1 + side, 3 * side, index % 3, None, True)
        return carry

    lax.fori_loop(0, 6, outer_density, 0)

    for copy in edge_copies:
        copy.wait()
    left_half = lane_ids(1) < SLOTS

    def edge_rows(edge):
        inside = jnp.where(gy == 0, 0.0, 1.0) if edge == 0 else jnp.where(gy == gy_count - 1, 0.0, 1.0)
        shift = -1.0 if edge == 0 else 1.0
        blocks = []
        for block in range(2):
            rows = []
            for f in range(7):
                if block == 0:
                    row = edge_got[edge, 0, f : f + 1, :]
                else:
                    right = edge_got[edge, 2, f : f + 1, :]
                    left = edge_got[edge, 1, f : f + 1, :]
                    if f == 0:
                        right = right + 2.0
                        left = left - 2.0
                    row = jnp.where(left_half, right, left)
                if f == 1:
                    row = row + shift
                if f == 3:
                    row = row * inside
                rows.append(row)
            blocks.append(rows)
        return blocks

    def edge_lane(edge):
        return 0 if edge == 0 else LANES - 1

    for edge in range(2):
        lane = edge_lane(edge)
        blocks = edge_rows(edge)
        for col in range(2):
            own_x, own_y, own_z = (near_p[1 + col, 1, f][:, lane : lane + 1] for f in range(3))
            total = jnp.zeros((SLOTS, LANES), F32)
            for rows in blocks:
                dist, spline = spline_of(own_x - rows[0], own_y - rows[1], own_z - rows[2])
                total = total + density_pair(dist, spline) * rows[3]
            summed = jnp.sum(total, axis=1, keepdims=True)
            rho_sum[col] += jnp.where(lane_ids(SLOTS) == lane, summed, 0.0)

    for slot, (col, shift) in enumerate(OTHERS):
        back = jnp.sum(rho_other[slot], axis=1)
        if shift != 0:
            back = jnp.where(lane_ids(SLOTS) == wrapped_lane(shift), 0.0, back)
        rho_sum[col] += shifted(back, -shift)

    for col in range(2):
        occupied = near_p[1 + col, 1, 3] > 0.0
        rho = (4.0 * KERNEL_NORM) * rho_sum[col]
        rho_out[pl.ds(col, SLOTS, stride=2), :] = jnp.where(occupied, rho, 0.0)
        rho = jnp.where(occupied, rho, 1.0)
        near_r[1 + col, 1, 0] = rho

    rho_copies = [
        send(10, near_r.at[1, 1, 0], got_r.at[1], -1, 0),
        send(11, near_r.at[2, 1, 0], got_r.at[0], 1, 0),
    ]
    own_rho = [[near_r[1 + col, 1, 0]] for col in range(2)]
    for edge, lane in ((0, 0), (1, LANES - 1)):
        edge_rho[edge] = edge_pack(own_rho, lane)
    edge_rho_copies = []
    for edge, step_y in ((0, -1), (1, 1)):
        for which, step_x in enumerate((0, 1, -1)):
            edge_rho_copies.append(
                send(12 + edge * 3 + which, edge_rho.at[edge], edge_rho_got.at[1 - edge, which], step_x, step_y)
            )

    def shift_rest(column, velocity, rho, first):
        for shift in (-1, 0, 1):
            if not (first and shift == 0):
                for f in range(3):
                    near_v[column, 1 + shift, f] = shifted(velocity[f], shift)
                near_r[column, 1 + shift, 0] = shifted(rho, shift)
            near_r[column, 1 + shift, 1] = pressure_term(shifted(rho, shift))

    for column in (1, 2):
        shift_rest(column, [near_v[column, 1, f] for f in range(3)], near_r[column, 1, 0], True)

    def strength_of(own, near, sep, dist_sq):
        closing = (near[4] - own[4]) * sep[0] + (near[5] - own[5]) * sep[1] + (near[6] - own[6]) * sep[2]
        damping = jnp.maximum(closing, 0.0) / ((dist_sq + 0.01 * SMOOTHING * SMOOTHING) * (own[7] + near[7]))
        return own[8] + near[8] + (2.0 * VISCOSITY) * damping

    def force_unit(unit, own_col, near_col, near_shift, other, fresh):
        def quarter(part, fresh_part):
            rows = pl.ds(pl.multiple_of(16 * part, 16), 16)
            own = (
                [near_p[own_col, 1, f, rows, :] for f in range(4)]
                + [near_v[own_col, 1, f, rows, :] for f in range(3)]
                + [near_r[own_col, 1, f, rows, :] for f in range(2)]
            )

            def step(j, totals):
                row = pl.ds(j, 1)
                near = (
                    [near_p[near_col, near_shift, f, row, :] for f in range(4)]
                    + [near_v[near_col, near_shift, f, row, :] for f in range(3)]
                    + [near_r[near_col, near_shift, f, row, :] for f in range(2)]
                )
                spline = kept[unit, j, rows, :]
                sep = [own[f] - near[f] for f in range(3)]
                dist = 1.0 - spline
                weight = strength_of(own, near, sep, dist * dist) * (spline * spline * spline) * near[3]
                if other is not None:
                    weight = weight * own[3]
                terms = [weight * sep[f] for f in range(3)]
                if other is not None:
                    for f in range(3):
                        back = terms[f][0:8] + terms[f][8:16]
                        if fresh_part:
                            force_other[f, other, j] = back
                        else:
                            force_other[f, other, j] += back
                return tuple(totals[f] + terms[f] for f in range(3))

            totals = lax.fori_loop(0, SLOTS, step, tuple(jnp.zeros((16, LANES), F32) for _ in range(3)), unroll=2)
            target = force_one if other is None else force_sum
            for f in range(3):
                target[own_col - 1, f, rows, :] += totals[f]

        if other is not None and fresh:
            quarter(0, True)
            lax.fori_loop(1, 4, lambda part, carry: (quarter(part, False), carry)[1], 0)
        else:
            lax.fori_loop(0, 4, lambda part, carry: (quarter(part, False), carry)[1], 0)

    force_sum[...] = jnp.zeros_like(force_sum)
    force_one[...] = jnp.zeros_like(force_one)
    seen = set()
    for unit, (own, near, shift, other) in enumerate(INNER):
        force_unit(unit, own, near, 1 + shift, other, other not in seen)
        seen.add(other)

    def self_force(col, carry):
        force_unit(len(INNER) + col, 1 + col, 1 + col, 1, None, True)
        return carry

    lax.fori_loop(0, 2, self_force, 0)

    for copy in vel_copies + rho_copies:
        copy.wait()
    for side in range(2):
        shift_rest(3 * side, [got_v[side, f] for f in range(3)], got_r[side], False)

    def outer_force(index, carry):
        side = index // 3
        force_unit(len(INNER) + 2 + index, 1 + side, 3 * side, index % 3, None, True)
        return carry

    lax.fori_loop(0, 6, outer_force, 0)

    for copy in edge_rho_copies:
        copy.wait()
    for edge in range(2):
        lane = edge_lane(edge)
        blocks = edge_rows(edge)
        for block in range(2):
            if block == 0:
                rho = edge_rho_got[edge, 0, 0:1, :]
            else:
                rho = jnp.where(left_half, edge_rho_got[edge, 2, 0:1, :], edge_rho_got[edge, 1, 0:1, :])
            blocks[block] = blocks[block] + [rho, pressure_term(rho)]
        for col in range(2):
            own = (
                [near_p[1 + col, 1, f][:, lane : lane + 1] for f in range(4)]
                + [near_v[1 + col, 1, f][:, lane : lane + 1] for f in range(3)]
                + [near_r[1 + col, 1, f][:, lane : lane + 1] for f in range(2)]
            )
            totals = [jnp.zeros((SLOTS, LANES), F32) for _ in range(3)]
            for near in blocks:
                sep = [own[f] - near[f] for f in range(3)]
                dist, spline = spline_of(*sep)
                weight = strength_of(own, near, sep, dist * dist) * (spline * spline * spline) * near[3]
                totals = [totals[f] + weight * sep[f] for f in range(3)]
            for f in range(3):
                summed = jnp.sum(totals[f], axis=1, keepdims=True)
                force_one[col, f] += jnp.where(lane_ids(SLOTS) == lane, summed, 0.0)

    for slot, (col, shift) in enumerate(OTHERS):
        for f in range(3):
            force_sum[col, f] -= shifted(jnp.sum(force_other[f, slot], axis=1), -shift)

    for col in range(2):
        rows = pl.ds(col, SLOTS, stride=2)
        mass = near_p[1 + col, 1, 3]
        occupied = mass > 0.0
        per_mass = 1.0 / jnp.where(occupied, mass, 1.0)
        row_id = (gy * LANES + lane_ids(SLOTS)).astype(F32)
        height = row_id + near_p[1 + col, 1, 1]
        near_floor = jnp.maximum(1.0 - 2.0 * height, 0.0)
        near_ceiling = jnp.maximum(1.0 - 2.0 * (float(LANES * gy_count) - height), 0.0)
        push = WALL_STIFFNESS * (near_floor * near_floor - near_ceiling * near_ceiling)
        for f in range(3):
            force = (20.0 * KERNEL_NORM) * (force_sum[col, f] * per_mass + force_one[col, f])
            if f == 1:
                force = force + push
            acc_out[f, rows, :] = jnp.where(occupied, force, 0.0)


def on_device(gx_count, gy_count, position, velocity, particle_mass, counts):
    vmem = pl.BlockSpec(memory_space=pltpu.VMEM)
    column = (SLOTS, LANES)
    rho, acceleration = pl.pallas_call(
        functools.partial(kernel, gx_count, gy_count),
        out_shape=(
            jax.ShapeDtypeStruct((2 * SLOTS, LANES), F32),
            jax.ShapeDtypeStruct((3, 2 * SLOTS, LANES), F32),
        ),
        in_specs=[vmem] * 4,
        out_specs=(vmem, vmem),
        scratch_shapes=[
            pltpu.VMEM((4, 3, 4) + column, F32),
            pltpu.VMEM((4, 3, 3) + column, F32),
            pltpu.VMEM((4, 3, 2) + column, F32),
            pltpu.VMEM((2, 4) + column, F32),
            pltpu.VMEM((2, 3) + column, F32),
            pltpu.VMEM((2,) + column, F32),
            pltpu.VMEM((2, 8, LANES), F32),
            pltpu.VMEM((2, 3, 8, LANES), F32),
            pltpu.VMEM((2, 8, LANES), F32),
            pltpu.VMEM((2, 3, 8, LANES), F32),
            pltpu.VMEM((UNITS, SLOTS) + column, F32),
            pltpu.VMEM((2,) + column, F32),
            pltpu.VMEM((4, SLOTS, 8, LANES), F32),
            pltpu.VMEM((2, 3) + column, F32),
            pltpu.VMEM((2, 3) + column, F32),
            pltpu.VMEM((3, 4, SLOTS, 8, LANES), F32),
            pltpu.SemaphoreType.DMA((18,)),
            pltpu.SemaphoreType.DMA((18,)),
        ],
        compiler_params=pltpu.CompilerParams(
            collective_id=0, has_side_effects=True, vmem_limit_bytes=52 * 1024 * 1024
        ),
        cost_estimate=pl.CostEstimate(flops=400_000_000, bytes_accessed=2_000_000, transcendentals=30_000_000),
    )(
        position.reshape(3, 2 * SLOTS, LANES),
        velocity.reshape(3, 2 * SLOTS, LANES),
        particle_mass.reshape(2 * SLOTS, LANES),
        counts,
    )
    return rho.reshape(SLOTS, 2, LANES), acceleration.reshape(3, SLOTS, 2, LANES)


def solution(mesh):
    in_specs = (
        P(None, None, "gx", "gy"),
        P(None, None, "gx", "gy"),
        P(None, "gx", "gy"),
        P("gx", "gy"),
    )
    out_specs = (P(None, "gx", "gy"), P(None, None, "gx", "gy"))
    step = functools.partial(on_device, mesh.shape["gx"], mesh.shape["gy"])
    return jax.shard_map(step, mesh=mesh, in_specs=in_specs, out_specs=out_specs, check_vma=False)
```

time: 259 us -> 101 us (0.39)
  other arithmetic: 112 us -> 0 us
  Pallas kernels: 0 us -> 94.4 us
  starting transfers between devices: 52 us -> 0 us
  local copies, waits for them, and re-layouts: 42.9 us -> 4.67 us
  loops' own time: 33.9 us -> 0 us
  waiting for transfers between devices: 14.7 us -> 0 us
    reduce_sum x48 -> x0, other arithmetic: 103 us -> none  [the longest x24 69.4 us: force_terms(): jnp.sum(pair_weight * sep_x, axis=1)]
    pallas_call x0 -> x1, Pallas kernels: none -> 94.4 us  [on_device(): pl.pallas_call(functools.partial(kernel, gx_count, gy_count), out_shape=(...]
    ppermute x8 -> x0, starting transfers between devices: 52 us -> none  [the longest x4 34.7 us: padded(): lax.ppermute(tail, axis, [(i, (i + 1) % count) for i in range(count)])]
    another operation x2 -> x0, loops' own time: 33.9 us -> none  [slot_blocks(): return lax.map(per_block, first_slots)]
    sub x32 -> x0, local copies, waits for them, and re-layouts: 16.5 us -> none  [the longest x16 8.85 us: force_kernel(): own_cells[3][:, None] - near_cells[3][None, :]]
    ppermute x8 -> x0, waiting for transfers between devices: 14.7 us -> none  [the longest x4 10.1 us: padded(): lax.ppermute(head, axis, [((i + 1) % count, i) for i in range(count)])]
    dynamic_slice x24 -> x0, local copies, waits for them, and re-layouts: 10.1 us -> none  [the longest x16 10 us: slot_blocks(): return lax.map(per_block, first_slots)]
    mul x32 -> x0, local copies, waits for them, and re-layouts: 7.71 us -> none  [the longest x24 5.12 us: force_terms(): pair_weight = near_cells[6][None, :] * strength]
  transfers between devices with their start and end apart: 8 -> 0, of which waited for: 5 -> 0; matrix products, arithmetic and copies ran while one was open for 1% -> 0% of each run, Pallas kernels for 0% -> 0%
where the time goes in v1:
time: 101 us; the launch traced here: 99.7 us
  Pallas kernels  94.4 us (93%)
  local copies, waits for them, and re-layouts  4.67 us (5%)
    pallas_call x1, Pallas kernels, on_device(): pl.pallas_call(functools.partial(kernel, gx_count, gy_count), out_shape=(...  94.4 us
    unnamed x10, local copies, waits for them, and re-layouts  4.67 us

profile of v1, /device:TPU:1, one launch (start us, length us, event | category | flops | bytes accessed | tf_op | source)
XLA Modules:
  0.0 99.7 jit_solution(13153916183768873292)
XLA Ops:
  0.6 0.0 copy-start.3
  0.6 0.7 copy-done.3
  1.3 0.0 copy-start
  1.3 0.9 copy-done
  2.2 0.0 copy-start.1
  2.2 0.9 copy-done.1
  3.2 0.0 copy-start.2
  3.2 0.8 copy-done.2
  4.0 94.4 %shard_map.59 = (f32[128,128]{1,0:T(8,128)S(1)}, f32[3,128,128]{2,1,0:T(8,128)S(1)}) custom-call(f32[3,128,128]{2,1,0:T(8,128)S(1)} %bitcast.7, f32[3,128,128]{2,1,0:T(8,128)S(1)} %bitcast.8, f32[128,128]{1,0:T(8,128)S(1)} %bitcast.9, s32[2,128]{1,0:T(2,128)S(1)} %copy-done.3), custom_call_target="tpu_custom_call" | custom-call | flops 400000000 | bytes 2000000 | tf_op jit(solution)/shard_map/pallas_call | solution.py:395
  98.4 0.6 copy.8
  99.1 0.7 copy.9
Async XLA Ops:
  0.6 0.7 copy-start.3
  1.3 0.9 copy-start
  2.2 0.9 copy-start.1
  3.2 0.8 copy-start.2

commit v2 on v1

v2 whole, which is shorter than its diff:
```python
import functools

import jax
import jax.numpy as jnp
from jax import lax
from jax.experimental import pallas as pl
from jax.experimental.pallas import tpu as pltpu
from jax.sharding import PartitionSpec as P

MESH = pl.DeviceIdType.MESH
F32 = jnp.float32
KERNEL_NORM = 21.0 / (2.0 * 3.141592653589793)
REST_DENSITY = 0.5
VISCOSITY = 0.5
SMOOTHING = 0.5
WALL_STIFFNESS = 4.0
TINY = 1e-30
SLOTS = 64
LANES = 128

OTHERS = ((0, 1), (1, -1), (1, 0), (1, 1), (2, -1), (2, 0), (2, 1), (0, 0))
SAME_ROW = (7, 2)
UNITS = 10
DENSITY_ROWS = 32
FORCE_ROWS = 16
DENSITY_UNROLL = 16
FORCE_UNROLL = 16


def pressure_term(rho):
    return (rho - REST_DENSITY) / (rho * rho)


def spline_of(dx, dy, dz):
    dist_sq = jnp.maximum(dx * dx + dy * dy + dz * dz, TINY)
    dist = dist_sq * lax.rsqrt(dist_sq)
    return dist, jnp.maximum(1.0 - dist, 0.0)


def density_pair(dist, spline):
    spline_sq = spline * spline
    return spline_sq * spline_sq * (dist + 0.25)


def strength_of(own, near, sep, dist_sq):
    closing = (near[4] - own[4]) * sep[0] + (near[5] - own[5]) * sep[1] + (near[6] - own[6]) * sep[2]
    damping = jnp.maximum(closing, 0.0) / ((dist_sq + 0.01 * SMOOTHING * SMOOTHING) * (own[7] + near[7]))
    return own[8] + near[8] + (2.0 * VISCOSITY) * damping


def lane_ids(rows):
    return lax.broadcasted_iota(jnp.int32, (rows, LANES), 1)


def shifted(cells, shift):
    return cells if shift == 0 else pltpu.roll(cells, (-shift) % LANES, 1)


def wrapped_lane(shift):
    return LANES - 1 if shift > 0 else 0


def groups_sum(cells):
    total = cells[0:8]
    for first in range(8, cells.shape[0], 8):
        total = total + cells[first : first + 8]
    return total


def kernel(
    gx_count, gy_count,
    pos_ref, vel_ref, mass_ref, counts_ref, rho_out, acc_out,
    near_p, near_v, near_r, got_p, got_v, got_r, back_d, got_d, back_f, got_f,
    edge_own, edge_got, edge_rho, edge_rho_got,
    kept, rho_sum, rho_other, force_sum, force_one, force_other, send_sem, recv_sem,
):
    gx = lax.axis_index("gx")
    gy = lax.axis_index("gy")

    def place(step_x, step_y):
        return (lax.rem(gx + step_x + gx_count, gx_count), lax.rem(gy + step_y + gy_count, gy_count))

    barrier = pltpu.get_barrier_semaphore()
    for step_x in (-1, 0, 1):
        for step_y in (-1, 0, 1):
            if step_x != 0 or step_y != 0:
                pl.semaphore_signal(barrier, inc=1, device_id=place(step_x, step_y), device_id_type=MESH)

    for col in range(2):
        rows = pl.ds(col, SLOTS, stride=2)
        slot = lax.broadcasted_iota(jnp.int32, (SLOTS, LANES), 0)
        occupied = slot < counts_ref[col : col + 1, :]
        near_p[col, 1, 0] = pos_ref[0, rows, :] + float(col)
        near_p[col, 1, 1] = pos_ref[1, rows, :]
        near_p[col, 1, 2] = pos_ref[2, rows, :]
        near_p[col, 1, 3] = jnp.where(occupied, mass_ref[rows, :], 0.0)

    pl.semaphore_wait(barrier, 8)

    def send(index, source, target, step_x, step_y):
        copy = pltpu.make_async_remote_copy(
            src_ref=source, dst_ref=target, send_sem=send_sem.at[index], recv_sem=recv_sem.at[index],
            device_id=place(step_x, step_y), device_id_type=MESH,
        )
        copy.start()
        return copy

    pos_copy = send(0, near_p.at[0, 1], got_p, -1, 0)

    for col in range(2):
        rows = pl.ds(col, SLOTS, stride=2)
        for axis in range(3):
            near_v[col, 1, axis] = SMOOTHING * vel_ref[axis, rows, :]

    def edge_pack(fields, lane):
        ids = lane_ids(SLOTS)
        halves = []
        for col in range(2):
            pack = jnp.zeros((SLOTS, LANES), F32)
            for index, field in enumerate(fields[col]):
                pack = jnp.where(ids == index, field[:, lane : lane + 1], pack)
            halves.append(pack)
        return jnp.concatenate(halves, axis=0).T[0:8, :]

    own_fields = [
        [near_p[col, 1, f] for f in range(4)] + [near_v[col, 1, f] for f in range(3)] for col in range(2)
    ]
    for edge, lane in ((0, 0), (1, LANES - 1)):
        edge_own[edge] = edge_pack(own_fields, lane)
    edge_copies = []
    for edge, step_y in ((0, -1), (1, 1)):
        for which, step_x in enumerate((0, 1, -1)):
            edge_copies.append(
                send(2 + edge * 3 + which, edge_own.at[edge], edge_got.at[1 - edge, which], step_x, step_y)
            )
    vel_copy = send(1, near_v.at[0, 1], got_v, -1, 0)

    rho_sum[...] = jnp.zeros_like(rho_sum)
    rho_other[...] = jnp.zeros_like(rho_other)
    force_sum[...] = jnp.zeros_like(force_sum)
    force_one[...] = jnp.zeros_like(force_one)
    force_other[...] = jnp.zeros_like(force_other)

    def shift_positions(column, columns, first):
        for shift in (-1, 0, 1):
            if first and shift == 0:
                continue
            ids = lane_ids(SLOTS)
            near_p[column, 1 + shift, 0] = shifted(columns[0], shift)
            near_p[column, 1 + shift, 1] = shifted(columns[1], shift) + float(shift)
            near_p[column, 1 + shift, 2] = shifted(columns[2], shift)
            mass = shifted(columns[3], shift)
            if shift != 0:
                mass = jnp.where(ids == wrapped_lane(shift), 0.0, mass)
            near_p[column, 1 + shift, 3] = mass

    for column in (0, 1):
        shift_positions(column, [near_p[column, 1, f] for f in range(4)], True)

    def density_block(unit, own, near, near_shift, other, first, count, near_first, near_last):
        rows = pl.ds(pl.multiple_of(first, 8), count)
        own_x, own_y, own_z, own_m = (near_p[own, 1, f, rows, :] for f in range(4))

        def step(j, total):
            near_x, near_y, near_z, near_m = (near_p[near, near_shift, f, pl.ds(j, 1), :] for f in range(4))
            dist, spline = spline_of(own_x - near_x, own_y - near_y, own_z - near_z)
            kept[unit, j, rows, :] = spline
            pair = density_pair(dist, spline)
            if other is not None:
                rho_other[other, pl.ds(pl.multiple_of(8 * j, 8), 8), :] += groups_sum(pair * own_m)
            return total + pair * near_m

        total = lax.fori_loop(near_first, near_last, step, jnp.zeros((count, LANES), F32), unroll=DENSITY_UNROLL)
        rho_sum[own, rows, :] += total

    def density_unit(unit, own, near, near_shift, other):
        def part(index, carry):
            density_block(unit, own, near, near_shift, other, index * DENSITY_ROWS, DENSITY_ROWS, 0, SLOTS)
            return carry

        lax.fori_loop(0, SLOTS // DENSITY_ROWS, part, 0)

    def each_same(block, rows):
        for col in range(2):
            for first in range(0, SLOTS, rows):
                block(col, col, col, 1, None, first, rows, first, first + rows)
                if first + rows < SLOTS:
                    block(col, col, col, 1, SAME_ROW[col], first, rows, first + rows, SLOTS)

    def other_sum(sums):
        total = sums[pl.ds(0, SLOTS, stride=8), :]
        for part in range(1, 8):
            total = total + sums[pl.ds(part, SLOTS, stride=8), :]
        return total

    def density_other(slot):
        shift = OTHERS[slot][1]
        back = other_sum(rho_other.at[slot])
        if shift != 0:
            back = jnp.where(lane_ids(SLOTS) == wrapped_lane(shift), 0.0, back)
        return shifted(back, -shift)

    each_same(density_block, FORCE_ROWS)
    density_unit(2, 0, 0, 2, 0)
    density_unit(3, 1, 1, 2, 3)

    pos_copy.wait()
    shift_positions(2, [got_p[0] + 2.0] + [got_p[f] for f in range(1, 4)], False)
    lax.fori_loop(0, 3, lambda k, carry: (density_unit(7 + k, 1, 2, k, 4 + k), carry)[1], 0)
    back_d[...] = density_other(4) + density_other(5) + density_other(6)
    back_d_copy = send(8, back_d, got_d, 1, 0)

    lax.fori_loop(0, 3, lambda k, carry: (density_unit(4 + k, 0, 1, k, 1 + k), carry)[1], 0)

    for copy in edge_copies:
        copy.wait()
    left_half = lane_ids(1) < SLOTS

    def edge_rows(edge):
        inside = jnp.where(gy == 0, 0.0, 1.0) if edge == 0 else jnp.where(gy == gy_count - 1, 0.0, 1.0)
        shift = -1.0 if edge == 0 else 1.0
        blocks = []
        for block in range(2):
            rows = []
            for f in range(7):
                if block == 0:
                    row = edge_got[edge, 0, f : f + 1, :]
                else:
                    right = edge_got[edge, 2, f : f + 1, :]
                    left = edge_got[edge, 1, f : f + 1, :]
                    if f == 0:
                        right = right + 2.0
                        left = left - 2.0
                    row = jnp.where(left_half, right, left)
                if f == 1:
                    row = row + shift
                if f == 3:
                    row = row * inside
                rows.append(row)
            blocks.append(rows)
        return blocks

    def edge_lane(edge):
        return 0 if edge == 0 else LANES - 1

    for edge in range(2):
        lane = edge_lane(edge)
        blocks = edge_rows(edge)
        for col in range(2):
            own_x, own_y, own_z = (near_p[col, 1, f][:, lane : lane + 1] for f in range(3))
            total = jnp.zeros((SLOTS, LANES), F32)
            for rows in blocks:
                dist, spline = spline_of(own_x - rows[0], own_y - rows[1], own_z - rows[2])
                total = total + density_pair(dist, spline) * rows[3]
            summed = jnp.sum(total, axis=1, keepdims=True)
            rho_sum[col] += jnp.where(lane_ids(SLOTS) == lane, summed, 0.0)

    for col in range(2):
        rho = rho_sum[col]
        for slot, (target, _) in enumerate(OTHERS):
            if target == col:
                rho = rho + density_other(slot)
        if col == 0:
            back_d_copy.wait()
            rho = rho + got_d[...]
        occupied = near_p[col, 1, 3] > 0.0
        rho = (4.0 * KERNEL_NORM) * rho
        rho_out[pl.ds(col, SLOTS, stride=2), :] = jnp.where(occupied, rho, 0.0)
        near_r[col, 1, 0] = jnp.where(occupied, rho, 1.0)

    rho_copy = send(9, near_r.at[0, 1, 0], got_r, -1, 0)
    own_rho = [[near_r[col, 1, 0]] for col in range(2)]
    for edge, lane in ((0, 0), (1, LANES - 1)):
        edge_rho[edge] = edge_pack(own_rho, lane)
    edge_rho_copies = []
    for edge, step_y in ((0, -1), (1, 1)):
        for which, step_x in enumerate((0, 1, -1)):
            edge_rho_copies.append(
                send(10 + edge * 3 + which, edge_rho.at[edge], edge_rho_got.at[1 - edge, which], step_x, step_y)
            )

    def shift_rest(column, velocity, rho, first):
        for shift in (-1, 0, 1):
            if not (first and shift == 0):
                for f in range(3):
                    near_v[column, 1 + shift, f] = shifted(velocity[f], shift)
                near_r[column, 1 + shift, 0] = shifted(rho, shift)
            near_r[column, 1 + shift, 1] = pressure_term(shifted(rho, shift))

    for column in (0, 1):
        shift_rest(column, [near_v[column, 1, f] for f in range(3)], near_r[column, 1, 0], True)

    def force_block(unit, own_col, near_col, near_shift, other, first, count, near_first, near_last):
        rows = pl.ds(pl.multiple_of(first, 8), count)
        own = (
            [near_p[own_col, 1, f, rows, :] for f in range(4)]
            + [near_v[own_col, 1, f, rows, :] for f in range(3)]
            + [near_r[own_col, 1, f, rows, :] for f in range(2)]
        )

        def step(j, totals):
            row = pl.ds(j, 1)
            near = (
                [near_p[near_col, near_shift, f, row, :] for f in range(4)]
                + [near_v[near_col, near_shift, f, row, :] for f in range(3)]
                + [near_r[near_col, near_shift, f, row, :] for f in range(2)]
            )
            spline = kept[unit, j, rows, :]
            sep = [own[f] - near[f] for f in range(3)]
            dist = 1.0 - spline
            weight = strength_of(own, near, sep, dist * dist) * (spline * spline * spline) * near[3]
            if other is not None:
                weight = weight * own[3]
            terms = [weight * sep[f] for f in range(3)]
            if other is not None:
                for f in range(3):
                    force_other[f, other, pl.ds(pl.multiple_of(8 * j, 8), 8), :] += groups_sum(terms[f])
            return tuple(totals[f] + terms[f] for f in range(3))

        zeros = tuple(jnp.zeros((count, LANES), F32) for _ in range(3))
        totals = lax.fori_loop(near_first, near_last, step, zeros, unroll=FORCE_UNROLL)
        target = force_one if other is None else force_sum
        for f in range(3):
            target[own_col, f, rows, :] += totals[f]

    def force_unit(unit, own, near, near_shift, other):
        def part(index, carry):
            force_block(unit, own, near, near_shift, other, index * FORCE_ROWS, FORCE_ROWS, 0, SLOTS)
            return carry

        lax.fori_loop(0, SLOTS // FORCE_ROWS, part, 0)

    def force_other_sum(f, slot):
        return shifted(other_sum(force_other.at[f, slot]), -OTHERS[slot][1])

    force_unit(2, 0, 0, 2, 0)
    force_unit(3, 1, 1, 2, 3)
    each_same(force_block, FORCE_ROWS)

    vel_copy.wait()
    rho_copy.wait()
    shift_rest(2, [got_v[f] for f in range(3)], got_r[...], False)
    lax.fori_loop(0, 3, lambda k, carry: (force_unit(7 + k, 1, 2, k, 4 + k), carry)[1], 0)
    for f in range(3):
        back_f[f] = force_other_sum(f, 4) + force_other_sum(f, 5) + force_other_sum(f, 6)
    back_f_copy = send(16, back_f, got_f, 1, 0)

    lax.fori_loop(0, 3, lambda k, carry: (force_unit(4 + k, 0, 1, k, 1 + k), carry)[1], 0)

    for copy in edge_rho_copies:
        copy.wait()
    for edge in range(2):
        lane = edge_lane(edge)
        blocks = edge_rows(edge)
        for block in range(2):
            if block == 0:
                rho = edge_rho_got[edge, 0, 0:1, :]
            else:
                rho = jnp.where(left_half, edge_rho_got[edge, 2, 0:1, :], edge_rho_got[edge, 1, 0:1, :])
            blocks[block] = blocks[block] + [rho, pressure_term(rho)]
        for col in range(2):
            own = (
                [near_p[col, 1, f][:, lane : lane + 1] for f in range(4)]
                + [near_v[col, 1, f][:, lane : lane + 1] for f in range(3)]
                + [near_r[col, 1, f][:, lane : lane + 1] for f in range(2)]
            )
            totals = [jnp.zeros((SLOTS, LANES), F32) for _ in range(3)]
            for near in blocks:
                sep = [own[f] - near[f] for f in range(3)]
                dist, spline = spline_of(*sep)
                weight = strength_of(own, near, sep, dist * dist) * (spline * spline * spline) * near[3]
                totals = [totals[f] + weight * sep[f] for f in range(3)]
            for f in range(3):
                summed = jnp.sum(totals[f], axis=1, keepdims=True)
                force_one[col, f] += jnp.where(lane_ids(SLOTS) == lane, summed, 0.0)

    for col in (1, 0):
        rows = pl.ds(col, SLOTS, stride=2)
        mass = near_p[col, 1, 3]
        occupied = mass > 0.0
        per_mass = 1.0 / jnp.where(occupied, mass, 1.0)
        row_id = (gy * LANES + lane_ids(SLOTS)).astype(F32)
        height = row_id + near_p[col, 1, 1]
        near_floor = jnp.maximum(1.0 - 2.0 * height, 0.0)
        near_ceiling = jnp.maximum(1.0 - 2.0 * (float(LANES * gy_count) - height), 0.0)
        push = WALL_STIFFNESS * (near_floor * near_floor - near_ceiling * near_ceiling)
        if col == 0:
            back_f_copy.wait()
        for f in range(3):
            both = force_sum[col, f]
            for slot, (target, _) in enumerate(OTHERS):
                if target == col:
                    both = both - force_other_sum(f, slot)
            if col == 0:
                both = both - got_f[f]
            force = (20.0 * KERNEL_NORM) * (both * per_mass + force_one[col, f])
            if f == 1:
                force = force + push
            acc_out[f, rows, :] = jnp.where(occupied, force, 0.0)


def on_device(gx_count, gy_count, position, velocity, particle_mass, counts):
    vmem = pl.BlockSpec(memory_space=pltpu.VMEM)
    column = (SLOTS, LANES)
    others = len(OTHERS)
    rho, acceleration = pl.pallas_call(
        functools.partial(kernel, gx_count, gy_count),
        out_shape=(
            jax.ShapeDtypeStruct((2 * SLOTS, LANES), F32),
            jax.ShapeDtypeStruct((3, 2 * SLOTS, LANES), F32),
        ),
        in_specs=[vmem] * 4,
        out_specs=(vmem, vmem),
        scratch_shapes=[
            pltpu.VMEM((3, 3, 4) + column, F32),
            pltpu.VMEM((3, 3, 3) + column, F32),
            pltpu.VMEM((3, 3, 2) + column, F32),
            pltpu.VMEM((4,) + column, F32),
            pltpu.VMEM((3,) + column, F32),
            pltpu.VMEM(column, F32),
            pltpu.VMEM(column, F32),
            pltpu.VMEM(column, F32),
            pltpu.VMEM((3,) + column, F32),
            pltpu.VMEM((3,) + column, F32),
            pltpu.VMEM((2, 8, LANES), F32),
            pltpu.VMEM((2, 3, 8, LANES), F32),
            pltpu.VMEM((2, 8, LANES), F32),
            pltpu.VMEM((2, 3, 8, LANES), F32),
            pltpu.VMEM((UNITS, SLOTS) + column, F32),
            pltpu.VMEM((2,) + column, F32),
            pltpu.VMEM((others, 8 * SLOTS, LANES), F32),
            pltpu.VMEM((2, 3) + column, F32),
            pltpu.VMEM((2, 3) + column, F32),
            pltpu.VMEM((3, others, 8 * SLOTS, LANES), F32),
            pltpu.SemaphoreType.DMA((17,)),
            pltpu.SemaphoreType.DMA((17,)),
        ],
        compiler_params=pltpu.CompilerParams(
            collective_id=0, has_side_effects=True, vmem_limit_bytes=52 * 1024 * 1024
        ),
        cost_estimate=pl.CostEstimate(flops=400_000_000, bytes_accessed=2_000_000, transcendentals=30_000_000),
    )(
        position.reshape(3, 2 * SLOTS, LANES),
        velocity.reshape(3, 2 * SLOTS, LANES),
        particle_mass.reshape(2 * SLOTS, LANES),
        counts,
    )
    return rho.reshape(SLOTS, 2, LANES), acceleration.reshape(3, SLOTS, 2, LANES)


def solution(mesh):
    in_specs = (
        P(None, None, "gx", "gy"),
        P(None, None, "gx", "gy"),
        P(None, "gx", "gy"),
        P("gx", "gy"),
    )
    out_specs = (P(None, "gx", "gy"), P(None, None, "gx", "gy"))
    step = functools.partial(on_device, mesh.shape["gx"], mesh.shape["gy"])
    return jax.shard_map(step, mesh=mesh, in_specs=in_specs, out_specs=out_specs, check_vma=False)
```

time: 101 us -> 70.8 us (0.70)
  Pallas kernels: 94.4 us -> 65.2 us
    pallas_call x1, Pallas kernels: 94.4 us -> 65.2 us  [on_device(): pl.pallas_call(functools.partial(kernel, gx_count, gy_count), out_shape=(...]
where the time goes in v2:
time: 70.8 us; the launch traced here: 70.5 us
  Pallas kernels  65.2 us (92%)
  local copies, waits for them, and re-layouts  4.67 us (7%)
    pallas_call x1, Pallas kernels, on_device(): pl.pallas_call(functools.partial(kernel, gx_count, gy_count), out_shape=(...  65.2 us
    unnamed x10, local copies, waits for them, and re-layouts  4.67 us

profile of v2, /device:TPU:1, one launch (start us, length us, event | category | flops | bytes accessed | tf_op | source)
XLA Modules:
  0.0 70.5 jit_solution(17932148315662735376)
XLA Ops:
  0.6 0.0 copy-start.3
  0.6 0.7 copy-done.3
  1.3 0.0 copy-start
  1.3 0.9 %copy-done = f32[3,64,2,128]{3,2,1,0:T(2,128)S(1)} copy-done((f32[3,64,2,128]{3,2,1,0:T(2,128)S(1)}, f32[3,64,2,128]{3,2,1,0:T(2,128)}, u32[]{:S(2)}) %copy-start) | copy-done | bytes 196632
  2.2 0.0 copy-start.1
  2.2 0.9 %copy-done.1 = f32[3,64,2,128]{3,2,1,0:T(2,128)S(1)} copy-done((f32[3,64,2,128]{3,2,1,0:T(2,128)S(1)}, f32[3,64,2,128]{3,2,1,0:T(2,128)}, u32[]{:S(2)}) %copy-start.1) | copy-done | bytes 196632
  3.2 0.0 copy-start.2
  3.2 0.8 %copy-done.2 = f32[64,2,128]{2,1,0:T(2,128)S(1)} copy-done((f32[64,2,128]{2,1,0:T(2,128)S(1)}, f32[64,2,128]{2,1,0:T(2,128)}, u32[]{:S(2)}) %copy-start.2) | copy-done | bytes 65560
  4.0 65.2 %shard_map.59 = (f32[128,128]{1,0:T(8,128)S(1)}, f32[3,128,128]{2,1,0:T(8,128)S(1)}) custom-call(f32[3,128,128]{2,1,0:T(8,128)S(1)} %bitcast.7, f32[3,128,128]{2,1,0:T(8,128)S(1)} %bitcast.8, f32[128,128]{1,0:T(8,128)S(1)} %bitcast.9, s32[2,128]{1,0:T(2,128)S(1)} %copy-done.3), custom_call_target="tpu_custom_call" | custom-call | flops 400000000 | bytes 2000000 | tf_op jit(solution)/shard_map/pallas_call | solution.py:406
  69.2 0.6 copy.8
  69.9 0.7 copy.9
Async XLA Ops:
  0.6 0.7 copy-start.3
  1.3 0.9 %copy-start = (f32[3,64,2,128]{3,2,1,0:T(2,128)S(1)}, f32[3,64,2,128]{3,2,1,0:T(2,128)}, u32[]{:S(2)}) copy-start(f32[3,64,2,128]{3,2,1,0:T(2,128)} %param.4) | copy-start | bytes 589828
  2.2 0.9 %copy-start.1 = (f32[3,64,2,128]{3,2,1,0:T(2,128)S(1)}, f32[3,64,2,128]{3,2,1,0:T(2,128)}, u32[]{:S(2)}) copy-start(f32[3,64,2,128]{3,2,1,0:T(2,128)} %param.5) | copy-start | bytes 589828
  3.2 0.8 %copy-start.2 = (f32[64,2,128]{2,1,0:T(2,128)S(1)}, f32[64,2,128]{2,1,0:T(2,128)}, u32[]{:S(2)}) copy-start(f32[64,2,128]{2,1,0:T(2,128)} %param.6) | copy-start | bytes 196612

commit v3 on v2

v3 whole, which is shorter than its diff:
```python
import functools

import jax
import jax.numpy as jnp
from jax import lax
from jax.experimental import pallas as pl
from jax.experimental.pallas import tpu as pltpu
from jax.sharding import PartitionSpec as P

MESH = pl.DeviceIdType.MESH
F32 = jnp.float32
KERNEL_NORM = 21.0 / (2.0 * 3.141592653589793)
REST_DENSITY = 0.5
VISCOSITY = 0.5
SMOOTHING = 0.5
WALL_STIFFNESS = 4.0
TINY = 1e-30
SLOTS = 64
LANES = 128

OTHERS = ((0, 1), (1, -1), (1, 0), (1, 1), (2, -1), (2, 0), (2, 1), (0, 0))
SAME_ROW = (7, 2)
INNER = 5
OUTER = 5
SAME = 8
UNITS = 10
SAME_ROWS = 16
JOINT_ROWS = 16
JOINT_UNROLL = 16
OUTER_ROWS = 32
OUTER_UNROLL = 16
FORCE_ROWS = 16
FORCE_UNROLL = 16
BEFORE_SEND = 3
BEFORE_PLACES = (5, 3)
BEFORE_DENSITY = (1, 0)
BEFORE_FORCE = (4, 0)
EPS = 0.01 * SMOOTHING * SMOOTHING
PACE = 2.0 * VISCOSITY * SMOOTHING


def pressure_term(rho):
    return (rho - REST_DENSITY) / (rho * rho)


def spline_of(sep):
    dist_sq = jnp.maximum(sep[0] * sep[0] + sep[1] * sep[1] + sep[2] * sep[2], TINY)
    dist = dist_sq * lax.rsqrt(dist_sq)
    return dist_sq, dist, jnp.maximum(1.0 - dist, 0.0)


def approach_of(own, near, sep, dist_sq):
    closing = (near[4] - own[4]) * sep[0] + (near[5] - own[5]) * sep[1] + (near[6] - own[6]) * sep[2]
    return jnp.maximum(closing, 0.0) / (dist_sq + EPS)


def lane_ids(rows):
    return lax.broadcasted_iota(jnp.int32, (rows, LANES), 1)


def shifted(cells, shift):
    return cells if shift == 0 else pltpu.roll(cells, (-shift) % LANES, 1)


def wrapped_lane(shift):
    return LANES - 1 if shift > 0 else 0


def groups_sum(cells):
    total = cells[0:8]
    for first in range(8, cells.shape[0], 8):
        total = total + cells[first : first + 8]
    return total


def other_rows(j):
    return pl.ds(pl.multiple_of(8 * j, 8), 8)


def kernel(
    gx_count, gy_count,
    pos_hbm, vel_hbm, mass_hbm, counts_hbm, rho_out, acc_out,
    pos_ref, vel_ref, mass_ref, counts_ref,
    near_p, near_v, near_r, got_p, got_v, got_r, back_d, got_d, back_f, got_f,
    edge_own, edge_got, edge_rho, edge_rho_got,
    kept_a, kept_b, rho_sum, rho_other, force_sum, force_other, send_sem, recv_sem, load_sem,
):
    gx = lax.axis_index("gx")
    gy = lax.axis_index("gy")
    early = lax.rem(gx, 2) == 0

    def steps(pair):
        return jnp.where(early, pair[0], pair[1])

    def place(step_x, step_y):
        return (lax.rem(gx + step_x + gx_count, gx_count), lax.rem(gy + step_y + gy_count, gy_count))

    barrier = pltpu.get_barrier_semaphore()
    for step_x in (-1, 0, 1):
        for step_y in (-1, 0, 1):
            if step_x != 0 or step_y != 0:
                pl.semaphore_signal(barrier, inc=1, device_id=place(step_x, step_y), device_id_type=MESH)

    loads = []
    for index, (source, target) in enumerate(
        ((pos_hbm, pos_ref), (counts_hbm, counts_ref), (mass_hbm, mass_ref), (vel_hbm, vel_ref))
    ):
        load = pltpu.make_async_copy(source, target, load_sem.at[index])
        load.start()
        loads.append(load)

    rho_sum[...] = jnp.zeros_like(rho_sum)
    rho_other[...] = jnp.zeros_like(rho_other)
    for load in loads[0:3]:
        load.wait()

    for col in range(2):
        rows = pl.ds(col, SLOTS, stride=2)
        slot = lax.broadcasted_iota(jnp.int32, (SLOTS, LANES), 0)
        occupied = slot < counts_ref[col : col + 1, :]
        near_p[col, 1, 0] = pos_ref[0, rows, :] + float(col)
        near_p[col, 1, 1] = pos_ref[1, rows, :]
        near_p[col, 1, 2] = pos_ref[2, rows, :]
        near_p[col, 1, 3] = jnp.where(occupied, mass_ref[rows, :], 0.0)
    loads[3].wait()
    for col in range(2):
        rows = pl.ds(col, SLOTS, stride=2)
        for axis in range(3):
            near_v[col, 1, axis] = PACE * vel_ref[axis, rows, :]

    def copy_of(index, source, target, step_x, step_y):
        return pltpu.make_async_remote_copy(
            src_ref=source, dst_ref=target, send_sem=send_sem.at[index], recv_sem=recv_sem.at[index],
            device_id=place(step_x, step_y), device_id_type=MESH,
        )

    def send(*args):
        copy = copy_of(*args)
        copy.start()
        return copy

    def edge_pack(fields, lane):
        ids = lane_ids(SLOTS)
        halves = []
        for col in range(2):
            pack = jnp.zeros((SLOTS, LANES), F32)
            for index, field in enumerate(fields[col]):
                pack = jnp.where(ids == index, field[:, lane : lane + 1], pack)
            halves.append(pack)
        return jnp.concatenate(halves, axis=0).T[0:8, :]

    def edge_sends(first, source, target):
        return [
            copy_of(first + edge * 3 + which, source.at[edge], target.at[1 - edge, which], step_x, step_y)
            for edge, step_y in ((0, -1), (1, 1))
            for which, step_x in enumerate((0, 1, -1))
        ]

    own_fields = [
        [near_p[col, 1, f] for f in range(4)] + [near_v[col, 1, f] for f in range(3)] for col in range(2)
    ]

    pos_copy = copy_of(0, near_p.at[1, 1], got_p, 1, 0)
    edge_copies = edge_sends(2, edge_own, edge_got)

    def exchange():
        pl.semaphore_wait(barrier, 8)
        pos_copy.start()
        for edge, lane in ((0, 0), (1, LANES - 1)):
            edge_own[edge] = edge_pack(own_fields, lane)
        for copy in edge_copies:
            copy.start()

    pl.when(jnp.logical_not(early))(exchange)

    def shift_positions(column, columns, first):
        for shift in (-1, 0, 1):
            if first and shift == 0:
                continue
            near_p[column, 1 + shift, 0] = shifted(columns[0], shift)
            near_p[column, 1 + shift, 1] = shifted(columns[1], shift) + float(shift)
            near_p[column, 1 + shift, 2] = shifted(columns[2], shift)
            mass = shifted(columns[3], shift)
            if shift != 0:
                mass = jnp.where(lane_ids(SLOTS) == wrapped_lane(shift), 0.0, mass)
            near_p[column, 1 + shift, 3] = mass

    def shift_velocities(column, columns, first):
        for shift in (-1, 0, 1):
            if not (first and shift == 0):
                for f in range(3):
                    near_v[column, 1 + shift, f] = shifted(columns[f], shift)

    for column in (0, 1):
        shift_positions(column, [near_p[column, 1, f] for f in range(4)], True)
        shift_velocities(column, [near_v[column, 1, f] for f in range(3)], True)

    def fields_of(refs, column, shift, rows):
        return [ref[column, shift, f, rows, :] for ref, count in refs for f in range(count)]

    places = ((near_p, 4),)
    moving = ((near_p, 4), (near_v, 3))

    def pair_block(unit, own_col, near_col, near_shift, other, first, count, near_first, near_count, joint, unroll):
        rows = pl.ds(pl.multiple_of(first, 8), count)
        refs = moving if joint else places
        own = fields_of(refs, own_col, 1, rows)

        def step(index, total):
            j = near_first + index
            near = fields_of(refs, near_col, near_shift, pl.ds(j, 1))
            sep = [own[f] - near[f] for f in range(3)]
            dist_sq, dist, spline = spline_of(sep)
            spline_sq = spline * spline
            both = own[3] * near[3]
            if joint:
                slope = spline_sq * spline * both
                pair = slope * (spline * (dist + 0.25))
                kept_a[unit, j, rows, :] = slope
                kept_b[unit, j, rows, :] = slope * approach_of(own, near, sep, dist_sq)
            else:
                pair = spline_sq * spline_sq * (dist + 0.25) * both
                kept_a[unit, j, rows, :] = spline
            if other is not None:
                rho_other[other, other_rows(j), :] += groups_sum(pair)
            return total + pair

        total = lax.fori_loop(0, near_count, step, jnp.zeros((count, LANES), F32), unroll=unroll)
        rho_sum[own_col, rows, :] += total

    def joint_block(unit, own, near, near_shift, other, first, count, near_first, near_count):
        pair_block(unit, own, near, near_shift, other, first, count, near_first, near_count, True, JOINT_UNROLL)

    def late_block(unit, own_col, near_col, near_shift, first, count):
        rows = pl.ds(pl.multiple_of(first, 8), count)
        own = fields_of(moving, own_col, 1, rows)

        def step(j, carry):
            near = fields_of(moving, near_col, near_shift, pl.ds(j, 1))
            sep = [own[f] - near[f] for f in range(3)]
            spline = kept_a[unit, j, rows, :]
            dist = 1.0 - spline
            slope = spline * spline * spline * (own[3] * near[3])
            kept_a[unit, j, rows, :] = slope
            kept_b[unit, j, rows, :] = slope * approach_of(own, near, sep, dist * dist)
            return carry

        lax.fori_loop(0, SLOTS, step, 0, unroll=JOINT_UNROLL)

    def each_part(rows, block, *args):
        def part(index, carry):
            block(*args, index * rows, rows)
            return carry

        lax.fori_loop(0, SLOTS // rows, part, 0)

    def same_cells(first_col, last_col, block):
        def in_part(part, col):
            first = SAME_ROWS * part
            block(SAME + col, col, col, 1, None, first, SAME_ROWS, first, SAME_ROWS)
            return col

        def in_pair(pair, col):
            part = jnp.where(pair < 3, 0, jnp.where(pair < 5, 1, 2))
            near = pair + 1 - jnp.where(pair < 3, 0, 2) - jnp.where(pair < 5, 0, 1)
            other = jnp.where(col == 0, SAME_ROW[0], SAME_ROW[1])
            block(SAME + col, col, col, 1, other, SAME_ROWS * part, SAME_ROWS, SAME_ROWS * near, SAME_ROWS)
            return col

        def column(col, carry):
            lax.fori_loop(0, SLOTS // SAME_ROWS, in_part, col)
            lax.fori_loop(0, 6, in_pair, col)
            return carry

        lax.fori_loop(first_col, last_col, column, 0)

    def inner_place(k):
        own = jnp.where(k == 1, 1, 0)
        near = jnp.where(k == 0, 0, 1)
        shift = jnp.where(k < 2, 2, k - 2)
        other = jnp.where(k == 0, 0, jnp.where(k == 1, 3, k - 1))
        return own, near, shift, other

    def inner_units(first, last, rows, block):
        def unit(k, carry):
            each_part(rows, lambda *args: block(*args, 0, SLOTS), k, *inner_place(k))
            return carry

        lax.fori_loop(first, last, unit, 0)

    def outer_units(first, last, rows, block):
        def unit(k, carry):
            each_part(rows, block, OUTER + k, 0, 2, k, 4 + k)
            return carry

        lax.fori_loop(first, last, unit, 0)

    def other_sum(sums):
        total = sums[pl.ds(0, SLOTS, stride=8), :]
        for part in range(1, 8):
            total = total + sums[pl.ds(part, SLOTS, stride=8), :]
        return total

    def others_of(sums, column):
        total = None
        for slot, (target, shift) in enumerate(OTHERS):
            if target == column:
                back = shifted(other_sum(sums.at[slot]), -shift)
                total = back if total is None else total + back
        return total

    vel_copy = copy_of(1, near_v.at[1, 1], got_v, 1, 0)

    same_cells(0, 2, joint_block)
    inner_units(0, 1, JOINT_ROWS, joint_block)
    pl.when(jnp.logical_not(early))(vel_copy.start)
    sent = steps((BEFORE_SEND, 1))
    inner_units(1, sent, JOINT_ROWS, joint_block)
    pl.when(early)(exchange)
    ahead = steps(BEFORE_PLACES)
    inner_units(sent, ahead, JOINT_ROWS, joint_block)

    pl.when(early)(vel_copy.start)
    pos_copy.wait()
    shift_positions(2, [got_p[0] - 2.0] + [got_p[f] for f in range(1, 4)], False)
    outer_units(0, 3, OUTER_ROWS, lambda *args: pair_block(*args, 0, SLOTS, False, OUTER_UNROLL))
    back_d[...] = others_of(rho_other, 2)
    back_d_copy = send(8, back_d, got_d, -1, 0)

    inner_units(ahead, INNER, JOINT_ROWS, joint_block)

    for copy in edge_copies:
        copy.wait()
    left_half = lane_ids(1) < SLOTS

    def edge_rows(edge):
        inside = jnp.where(gy == 0, 0.0, 1.0) if edge == 0 else jnp.where(gy == gy_count - 1, 0.0, 1.0)
        shift = -1.0 if edge == 0 else 1.0
        blocks = []
        for block in range(2):
            rows = []
            for f in range(7):
                if block == 0:
                    row = edge_got[edge, 0, f : f + 1, :]
                else:
                    right = edge_got[edge, 2, f : f + 1, :]
                    left = edge_got[edge, 1, f : f + 1, :]
                    if f == 0:
                        right = right + 2.0
                        left = left - 2.0
                    row = jnp.where(left_half, right, left)
                if f == 1:
                    row = row + shift
                if f == 3:
                    row = row * inside
                rows.append(row)
            blocks.append(rows)
        return blocks

    def edge_lane(edge):
        return 0 if edge == 0 else LANES - 1

    def at_edge(total, col, lane):
        summed = jnp.sum(total, axis=1, keepdims=True) * near_p[col, 1, 3]
        return jnp.where(lane_ids(SLOTS) == lane, summed, 0.0)

    for edge in range(2):
        lane = edge_lane(edge)
        blocks = edge_rows(edge)
        for col in range(2):
            own = [near_p[col, 1, f][:, lane : lane + 1] for f in range(3)]
            total = jnp.zeros((SLOTS, LANES), F32)
            for near in blocks:
                _, dist, spline = spline_of([own[f] - near[f] for f in range(3)])
                spline_sq = spline * spline
                total = total + spline_sq * spline_sq * (dist + 0.25) * near[3]
            rho_sum[col] += at_edge(total, col, lane)

    def shift_densities(column, rho, first):
        for shift in (-1, 0, 1):
            if not (first and shift == 0):
                near_r[column, 1 + shift, 0] = shifted(rho, shift)
            near_r[column, 1 + shift, 1] = pressure_term(shifted(rho, shift))

    def occupied_of(col):
        mass = near_p[col, 1, 3]
        occupied = mass > 0.0
        return occupied, 1.0 / jnp.where(occupied, mass, 1.0)

    def finish_density(col, more):
        occupied, per_mass = occupied_of(col)
        rho = rho_sum[col] + others_of(rho_other, col)
        if more is not None:
            rho = rho + more
        rho = (4.0 * KERNEL_NORM) * rho * per_mass
        rho_out[pl.ds(col, SLOTS, stride=2), :] = jnp.where(occupied, rho, 0.0)
        near_r[col, 1, 0] = jnp.where(occupied, rho, 1.0)

    force_sum[...] = jnp.zeros_like(force_sum)
    force_other[...] = jnp.zeros_like(force_other)

    def force_block(unit, own_col, near_col, near_shift, other, first, count, near_first, near_count):
        rows = pl.ds(pl.multiple_of(first, 8), count)
        own = [near_p[own_col, 1, f, rows, :] for f in range(3)] + [near_r[own_col, 1, f, rows, :] for f in range(2)]

        def step(index, totals):
            j = near_first + index
            row = pl.ds(j, 1)
            near = [near_p[near_col, near_shift, f, row, :] for f in range(3)]
            near += [near_r[near_col, near_shift, f, row, :] for f in range(2)]
            weight = kept_a[unit, j, rows, :] * (own[4] + near[4])
            weight = weight + kept_b[unit, j, rows, :] / (own[3] + near[3])
            terms = [weight * (own[f] - near[f]) for f in range(3)]
            if other is not None:
                for f in range(3):
                    force_other[f, other, other_rows(j), :] += groups_sum(terms[f])
            return tuple(totals[f] + terms[f] for f in range(3))

        zeros = tuple(jnp.zeros((count, LANES), F32) for _ in range(3))
        totals = lax.fori_loop(0, near_count, step, zeros, unroll=FORCE_UNROLL)
        for f in range(3):
            force_sum[own_col, f, rows, :] += totals[f]

    def late_units(first, last):
        outer_units(
            first, last, JOINT_ROWS,
            lambda unit, own, near, shift, other, start, count: late_block(unit, own, near, shift, start, count),
        )

    finish_density(0, None)
    shift_densities(0, near_r[0, 1, 0], True)
    vel_copy.wait()
    shift_velocities(2, [got_v[f] for f in range(3)], False)
    done = steps(BEFORE_DENSITY)
    one = steps((1, 0))
    same_cells(0, one, force_block)
    inner_units(0, one, FORCE_ROWS, force_block)
    late_units(0, done)

    back_d_copy.wait()
    finish_density(1, got_d[...])
    rho_copy = send(9, near_r.at[1, 1, 0], got_r, 1, 0)
    own_rho = [[near_r[col, 1, 0]] for col in range(2)]
    for edge, lane in ((0, 0), (1, LANES - 1)):
        edge_rho[edge] = edge_pack(own_rho, lane)
    edge_rho_copies = edge_sends(10, edge_rho, edge_rho_got)
    for copy in edge_rho_copies:
        copy.start()
    shift_densities(1, near_r[1, 1, 0], True)

    late_units(done, 3)
    two = steps((2, 0))
    ahead = steps(BEFORE_FORCE)
    same_cells(one, two, force_block)
    inner_units(one, ahead, FORCE_ROWS, force_block)

    rho_copy.wait()
    shift_densities(2, got_r[...], False)
    outer_units(0, 3, FORCE_ROWS, lambda *args: force_block(*args, 0, SLOTS))
    for f in range(3):
        back_f[f] = others_of(force_other.at[f], 2)
    back_f_copy = send(16, back_f, got_f, -1, 0)

    same_cells(two, 2, force_block)
    inner_units(ahead, INNER, FORCE_ROWS, force_block)

    for copy in edge_rho_copies:
        copy.wait()
    for edge in range(2):
        lane = edge_lane(edge)
        blocks = edge_rows(edge)
        for block in range(2):
            if block == 0:
                rho = edge_rho_got[edge, 0, 0:1, :]
            else:
                rho = jnp.where(left_half, edge_rho_got[edge, 2, 0:1, :], edge_rho_got[edge, 1, 0:1, :])
            blocks[block] = blocks[block] + [rho, pressure_term(rho)]
        for col in range(2):
            own = [ref[col, 1, f][:, lane : lane + 1] for ref, n in ((near_p, 4), (near_v, 3), (near_r, 2)) for f in range(n)]
            totals = [jnp.zeros((SLOTS, LANES), F32) for _ in range(3)]
            for near in blocks:
                sep = [own[f] - near[f] for f in range(3)]
                dist_sq, _, spline = spline_of(sep)
                strength = own[8] + near[8] + approach_of(own, near, sep, dist_sq) / (own[7] + near[7])
                weight = strength * (spline * spline * spline) * near[3]
                totals = [totals[f] + weight * sep[f] for f in range(3)]
            for f in range(3):
                force_sum[col, f] += at_edge(totals[f], col, lane)

    for col in (0, 1):
        rows = pl.ds(col, SLOTS, stride=2)
        occupied, per_mass = occupied_of(col)
        row_id = (gy * LANES + lane_ids(SLOTS)).astype(F32)
        height = row_id + near_p[col, 1, 1]
        near_floor = jnp.maximum(1.0 - 2.0 * height, 0.0)
        near_ceiling = jnp.maximum(1.0 - 2.0 * (float(LANES * gy_count) - height), 0.0)
        push = WALL_STIFFNESS * (near_floor * near_floor - near_ceiling * near_ceiling)
        sums = [force_sum[col, f] - others_of(force_other.at[f], col) for f in range(3)]
        if col == 1:
            back_f_copy.wait()
            sums = [sums[f] - got_f[f] for f in range(3)]
        for f in range(3):
            force = (20.0 * KERNEL_NORM) * sums[f] * per_mass
            if f == 1:
                force = force + push
            acc_out[f, rows, :] = jnp.where(occupied, force, 0.0)


def on_device(gx_count, gy_count, position, velocity, particle_mass, counts):
    vmem = pl.BlockSpec(memory_space=pltpu.VMEM)
    anywhere = pl.BlockSpec(memory_space=pl.ANY)
    column = (SLOTS, LANES)
    others = len(OTHERS)
    rho, acceleration = pl.pallas_call(
        functools.partial(kernel, gx_count, gy_count),
        out_shape=(
            jax.ShapeDtypeStruct((2 * SLOTS, LANES), F32),
            jax.ShapeDtypeStruct((3, 2 * SLOTS, LANES), F32),
        ),
        in_specs=[anywhere] * 4,
        out_specs=(vmem, vmem),
        scratch_shapes=[
            pltpu.VMEM((3, 2 * SLOTS, LANES), F32),
            pltpu.VMEM((3, 2 * SLOTS, LANES), F32),
            pltpu.VMEM((2 * SLOTS, LANES), F32),
            pltpu.VMEM((2, LANES), jnp.int32),
            pltpu.VMEM((3, 3, 4) + column, F32),
            pltpu.VMEM((3, 3, 3) + column, F32),
            pltpu.VMEM((3, 3, 2) + column, F32),
            pltpu.VMEM((4,) + column, F32),
            pltpu.VMEM((3,) + column, F32),
            pltpu.VMEM(column, F32),
            pltpu.VMEM(column, F32),
            pltpu.VMEM(column, F32),
            pltpu.VMEM((3,) + column, F32),
            pltpu.VMEM((3,) + column, F32),
            pltpu.VMEM((2, 8, LANES), F32),
            pltpu.VMEM((2, 3, 8, LANES), F32),
            pltpu.VMEM((2, 8, LANES), F32),
            pltpu.VMEM((2, 3, 8, LANES), F32),
            pltpu.VMEM((UNITS, SLOTS) + column, F32),
            pltpu.VMEM((UNITS, SLOTS) + column, F32),
            pltpu.VMEM((2,) + column, F32),
            pltpu.VMEM((others, 8 * SLOTS, LANES), F32),
            pltpu.VMEM((2, 3) + column, F32),
            pltpu.VMEM((3, others, 8 * SLOTS, LANES), F32),
            pltpu.SemaphoreType.DMA((17,)),
            pltpu.SemaphoreType.DMA((17,)),
            pltpu.SemaphoreType.DMA((4,)),
        ],
        compiler_params=pltpu.CompilerParams(
            collective_id=0, has_side_effects=True, vmem_limit_bytes=58 * 1024 * 1024
        ),
        cost_estimate=pl.CostEstimate(flops=400_000_000, bytes_accessed=2_000_000, transcendentals=30_000_000),
    )(
        position.reshape(3, 2 * SLOTS, LANES),
        velocity.reshape(3, 2 * SLOTS, LANES),
        particle_mass.reshape(2 * SLOTS, LANES),
        counts,
    )
    return rho.reshape(SLOTS, 2, LANES), acceleration.reshape(3, SLOTS, 2, LANES)


def solution(mesh):
    in_specs = (
        P(None, None, "gx", "gy"),
        P(None, None, "gx", "gy"),
        P(None, "gx", "gy"),
        P("gx", "gy"),
    )
    out_specs = (P(None, "gx", "gy"), P(None, None, "gx", "gy"))
    step = functools.partial(on_device, mesh.shape["gx"], mesh.shape["gy"])
    return jax.shard_map(step, mesh=mesh, in_specs=in_specs, out_specs=out_specs, check_vma=False)
```

time: 70.8 us -> 57.6 us (0.81)
  the two profiles are of different devices: /device:TPU:1 before, /device:TPU:256 now
where the time goes in v3:
time: 57.6 us; the launch traced here: 57.4 us
  Pallas kernels  53.7 us (93%)
  local copies, waits for them, and re-layouts  3.09 us (5%)
  between operations  0.64 us (1%)
    pallas_call x1, Pallas kernels, on_device(): pl.pallas_call(functools.partial(kernel, gx_count, gy_count), out_shape=(...  53.7 us
    unnamed x2, local copies, waits for them, and re-layouts  3.09 us

profile of v3, /device:TPU:256, one launch (start us, length us, event | category | flops | bytes accessed | tf_op | source)
XLA Modules:
  0.0 57.4 jit_solution(11058879418318839569)
XLA Ops:
  0.6 53.7 %shard_map.59 = (f32[128,128]{1,0:T(8,128)}, f32[3,128,128]{2,1,0:T(8,128)}) custom-call(f32[3,128,128]{2,1,0:T(8,128)} %bitcast.7, f32[3,128,128]{2,1,0:T(8,128)} %bitcast.8, f32[128,128]{1,0:T(8,128)} %bitcast.9, s32[2,128]{1,0:T(2,128)} %counts_hbm.1), custom_call_target="tpu_custom_call" | custom-call | flops 400000000 | bytes 2000000 | tf_op jit(solution)/shard_map/pallas_call | solution.py:514
  54.3 1.5 %copy.8 = f32[64,2,128]{2,1,0:T(2,128)} copy(f32[64,2,128]{2,1,0:T(2,128)} %bitcast.6) | data formatting | bytes 131072
  55.8 1.6 %copy.9 = f32[3,64,2,128]{3,2,1,0:T(2,128)} copy(f32[3,64,2,128]{3,2,1,0:T(2,128)} %bitcast.5) | data formatting | bytes 393216

commit v4 on v3

--- a/solution.py
+++ b/solution.py
@@ -17,6 +17,7 @@
 TINY = 1e-30
 SLOTS = 64
 LANES = 128
+HALF = SLOTS // 2
 
 OTHERS = ((0, 1), (1, -1), (1, 0), (1, 1), (2, -1), (2, 0), (2, 1), (0, 0))
 SAME_ROW = (7, 2)
@@ -31,10 +32,10 @@
 OUTER_UNROLL = 16
 FORCE_ROWS = 16
 FORCE_UNROLL = 16
-BEFORE_SEND = 3
-BEFORE_PLACES = (5, 3)
+BEFORE_SEND = (1, 1)
+BEFORE_PLACES = (5, 2)
 BEFORE_DENSITY = (1, 0)
-BEFORE_FORCE = (4, 0)
+BEFORE_FORCE = (5, 0)
 EPS = 0.01 * SMOOTHING * SMOOTHING
 PACE = 2.0 * VISCOSITY * SMOOTHING
 
@@ -83,7 +84,7 @@
     pos_ref, vel_ref, mass_ref, counts_ref,
     near_p, near_v, near_r, got_p, got_v, got_r, back_d, got_d, back_f, got_f,
     edge_own, edge_got, edge_rho, edge_rho_got,
-    kept_a, kept_b, rho_sum, rho_other, force_sum, force_other, send_sem, recv_sem, load_sem,
+    kept_a, kept_b, rho_sum, rho_other, force_sum, force_other, send_sem, recv_sem, load_sem, left_sem,
 ):
     gx = lax.axis_index("gx")
     gy = lax.axis_index("gy")
@@ -96,10 +97,14 @@
         return (lax.rem(gx + step_x + gx_count, gx_count), lax.rem(gy + step_y + gy_count, gy_count))
 
     barrier = pltpu.get_barrier_semaphore()
-    for step_x in (-1, 0, 1):
-        for step_y in (-1, 0, 1):
-            if step_x != 0 or step_y != 0:
-                pl.semaphore_signal(barrier, inc=1, device_id=place(step_x, step_y), device_id_type=MESH)
+    for step_x, step_y in ((-1, 0), (-1, -1), (-1, 1), (0, -1), (0, 1)):
+        pl.semaphore_signal(barrier, inc=1, device_id=place(step_x, step_y), device_id_type=MESH)
+
+    @pl.when(early)
+    def _():
+        for step_y in (0, -1, 1):
+            pl.semaphore_signal(barrier, inc=1, device_id=place(1, step_y), device_id_type=MESH)
+
 
     loads = []
     for index, (source, target) in enumerate(
@@ -109,12 +114,27 @@
         load.start()
         loads.append(load)
 
-    rho_sum[...] = jnp.zeros_like(rho_sum)
-    rho_other[...] = jnp.zeros_like(rho_other)
     for load in loads[0:3]:
         load.wait()
 
-    for col in range(2):
+    def copy_of(index, source, target, step_x, step_y):
+        return pltpu.make_async_remote_copy(
+            src_ref=source, dst_ref=target, send_sem=send_sem.at[index], recv_sem=recv_sem.at[index],
+            device_id=place(step_x, step_y), device_id_type=MESH,
+        )
+
+    def send(*args):
+        copy = copy_of(*args)
+        copy.start()
+        return copy
+
+    pos_copy = copy_of(0, near_p.at[1, 1], got_p, 1, 0)
+
+    def enter():
+        pl.semaphore_wait(barrier, steps((5, 8)))
+        pos_copy.start()
+
+    for col in (1, 0):
         rows = pl.ds(col, SLOTS, stride=2)
         slot = lax.broadcasted_iota(jnp.int32, (SLOTS, LANES), 0)
         occupied = slot < counts_ref[col : col + 1, :]
@@ -122,22 +142,15 @@
         near_p[col, 1, 1] = pos_ref[1, rows, :]
         near_p[col, 1, 2] = pos_ref[2, rows, :]
         near_p[col, 1, 3] = jnp.where(occupied, mass_ref[rows, :], 0.0)
+        if col == 1:
+            pl.when(jnp.logical_not(early))(enter)
+    rho_sum[...] = jnp.zeros_like(rho_sum)
+    rho_other[...] = jnp.zeros_like(rho_other)
     loads[3].wait()
     for col in range(2):
         rows = pl.ds(col, SLOTS, stride=2)
         for axis in range(3):
             near_v[col, 1, axis] = PACE * vel_ref[axis, rows, :]
-
-    def copy_of(index, source, target, step_x, step_y):
-        return pltpu.make_async_remote_copy(
-            src_ref=source, dst_ref=target, send_sem=send_sem.at[index], recv_sem=recv_sem.at[index],
-            device_id=place(step_x, step_y), device_id_type=MESH,
-        )
-
-    def send(*args):
-        copy = copy_of(*args)
-        copy.start()
-        return copy
 
     def edge_pack(fields, lane):
         ids = lane_ids(SLOTS)
@@ -160,18 +173,26 @@
         [near_p[col, 1, f] for f in range(4)] + [near_v[col, 1, f] for f in range(3)] for col in range(2)
     ]
 
-    pos_copy = copy_of(0, near_p.at[1, 1], got_p, 1, 0)
     edge_copies = edge_sends(2, edge_own, edge_got)
 
-    def exchange():
-        pl.semaphore_wait(barrier, 8)
-        pos_copy.start()
+    def pack_edges():
         for edge, lane in ((0, 0), (1, LANES - 1)):
             edge_own[edge] = edge_pack(own_fields, lane)
+
+    def start_early():
+        enter()
+        pack_edges()
+        for index in (0, 1, 3, 4):
+            edge_copies[index].start()
+
+    def start_late():
+        for step_y in (0, -1, 1):
+            pl.semaphore_signal(left_sem, inc=1, device_id=place(1, step_y), device_id_type=MESH)
+        pack_edges()
         for copy in edge_copies:
             copy.start()
 
-    pl.when(jnp.logical_not(early))(exchange)
+    pl.when(jnp.logical_not(early))(start_late)
 
     def shift_positions(column, columns, first):
         for shift in (-1, 0, 1):
@@ -295,17 +316,17 @@
 
         lax.fori_loop(first, last, unit, 0)
 
-    def other_sum(sums):
-        total = sums[pl.ds(0, SLOTS, stride=8), :]
+    def other_sum(sums, first, count):
+        total = sums[pl.ds(8 * first, count, stride=8), :]
         for part in range(1, 8):
-            total = total + sums[pl.ds(part, SLOTS, stride=8), :]
+            total = total + sums[pl.ds(8 * first + part, count, stride=8), :]
         return total
 
-    def others_of(sums, column):
+    def others_of(sums, column, first=0, count=SLOTS):
         total = None
         for slot, (target, shift) in enumerate(OTHERS):
             if target == column:
-                back = shifted(other_sum(sums.at[slot]), -shift)
+                back = shifted(other_sum(sums.at[slot], first, count), -shift)
                 total = back if total is None else total + back
         return total
 
@@ -313,15 +334,23 @@
 
     same_cells(0, 2, joint_block)
     inner_units(0, 1, JOINT_ROWS, joint_block)
-    pl.when(jnp.logical_not(early))(vel_copy.start)
-    sent = steps((BEFORE_SEND, 1))
+    sent = steps(BEFORE_SEND)
     inner_units(1, sent, JOINT_ROWS, joint_block)
-    pl.when(early)(exchange)
+    pl.when(early)(start_early)
     ahead = steps(BEFORE_PLACES)
     inner_units(sent, ahead, JOINT_ROWS, joint_block)
 
-    pl.when(early)(vel_copy.start)
+    force_sum[...] = jnp.zeros_like(force_sum)
+    force_other[...] = jnp.zeros_like(force_other)
     pos_copy.wait()
+    vel_copy.start()
+
+    @pl.when(early)
+    def _():
+        pl.semaphore_wait(left_sem, 3)
+        edge_copies[2].start()
+        edge_copies[5].start()
+
     shift_positions(2, [got_p[0] - 2.0] + [got_p[f] for f in range(1, 4)], False)
     outer_units(0, 3, OUTER_ROWS, lambda *args: pair_block(*args, 0, SLOTS, False, OUTER_UNROLL))
     back_d[...] = others_of(rho_other, 2)
@@ -396,8 +425,6 @@
         rho_out[pl.ds(col, SLOTS, stride=2), :] = jnp.where(occupied, rho, 0.0)
         near_r[col, 1, 0] = jnp.where(occupied, rho, 1.0)
 
-    force_sum[...] = jnp.zeros_like(force_sum)
-    force_other[...] = jnp.zeros_like(force_other)
 
     def force_block(unit, own_col, near_col, near_shift, other, first, count, near_first, near_count):
         rows = pl.ds(pl.multiple_of(first, 8), count)
@@ -429,12 +456,12 @@
 
     finish_density(0, None)
     shift_densities(0, near_r[0, 1, 0], True)
-    vel_copy.wait()
-    shift_velocities(2, [got_v[f] for f in range(3)], False)
     done = steps(BEFORE_DENSITY)
     one = steps((1, 0))
     same_cells(0, one, force_block)
     inner_units(0, one, FORCE_ROWS, force_block)
+    vel_copy.wait()
+    shift_velocities(2, [got_v[f] for f in range(3)], False)
     late_units(0, done)
 
     back_d_copy.wait()
@@ -456,10 +483,13 @@
 
     rho_copy.wait()
     shift_densities(2, got_r[...], False)
-    outer_units(0, 3, FORCE_ROWS, lambda *args: force_block(*args, 0, SLOTS))
-    for f in range(3):
-        back_f[f] = others_of(force_other.at[f], 2)
-    back_f_copy = send(16, back_f, got_f, -1, 0)
+    back_f_copies = []
+    for half in range(2):
+        first, count = HALF * half, HALF
+        outer_units(0, 3, FORCE_ROWS, lambda *args: force_block(*args, first, count))
+        for f in range(3):
+            back_f[half, f] = others_of(force_other.at[f], 2, first, count)
+        back_f_copies.append(send(16 + half, back_f.at[half], got_f.at[half], -1, 0))
 
     same_cells(two, 2, force_block)
     inner_units(ahead, INNER, FORCE_ROWS, force_block)
@@ -497,8 +527,9 @@
         push = WALL_STIFFNESS * (near_floor * near_floor - near_ceiling * near_ceiling)
         sums = [force_sum[col, f] - others_of(force_other.at[f], col) for f in range(3)]
         if col == 1:
-            back_f_copy.wait()
-            sums = [sums[f] - got_f[f] for f in range(3)]
+            for copy in back_f_copies:
+                copy.wait()
+            sums = [sums[f] - jnp.concatenate([got_f[0, f], got_f[1, f]], axis=0) for f in range(3)]
         for f in range(3):
             force = (20.0 * KERNEL_NORM) * sums[f] * per_mass
             if f == 1:
@@ -532,8 +563,8 @@
             pltpu.VMEM(column, F32),
             pltpu.VMEM(column, F32),
             pltpu.VMEM(column, F32),
-            pltpu.VMEM((3,) + column, F32),
-            pltpu.VMEM((3,) + column, F32),
+            pltpu.VMEM((2, 3, HALF, LANES), F32),
+            pltpu.VMEM((2, 3, HALF, LANES), F32),
             pltpu.VMEM((2, 8, LANES), F32),
             pltpu.VMEM((2, 3, 8, LANES), F32),
             pltpu.VMEM((2, 8, LANES), F32),
@@ -544,9 +575,10 @@
             pltpu.VMEM((others, 8 * SLOTS, LANES), F32),
             pltpu.VMEM((2, 3) + column, F32),
             pltpu.VMEM((3, others, 8 * SLOTS, LANES), F32),
-            pltpu.SemaphoreType.DMA((17,)),
-            pltpu.SemaphoreType.DMA((17,)),
+            pltpu.SemaphoreType.DMA((18,)),
+            pltpu.SemaphoreType.DMA((18,)),
             pltpu.SemaphoreType.DMA((4,)),
+            pltpu.SemaphoreType.REGULAR,
         ],
         compiler_params=pltpu.CompilerParams(
             collective_id=0, has_side_effects=True, vmem_limit_bytes=58 * 1024 * 1024

time: 57.6 us -> 54.9 us (0.953)
  the two profiles are of different devices: /device:TPU:256 before, /device:TPU:64 now
where the time goes in v4:
time: 54.9 us; the launch traced here: 54.7 us
  Pallas kernels  51 us (93%)
  local copies, waits for them, and re-layouts  3.09 us (6%)
  between operations  0.64 us (1%)
    pallas_call x1, Pallas kernels, on_device(): pl.pallas_call(functools.partial(kernel, gx_count, gy_count), out_shape=(...  51 us
    unnamed x2, local copies, waits for them, and re-layouts  3.09 us

profile of v4, /device:TPU:64, one launch (start us, length us, event | category | flops | bytes accessed | tf_op | source)
XLA Modules:
  0.0 54.7 jit_solution(8702192012614522512)
XLA Ops:
  0.6 51.0 %shard_map.59 = (f32[128,128]{1,0:T(8,128)}, f32[3,128,128]{2,1,0:T(8,128)}) custom-call(f32[3,128,128]{2,1,0:T(8,128)} %bitcast.7, f32[3,128,128]{2,1,0:T(8,128)} %bitcast.8, f32[128,128]{1,0:T(8,128)} %bitcast.9, s32[2,128]{1,0:T(2,128)} %counts_hbm.1), custom_call_target="tpu_custom_call" | custom-call | flops 400000000 | bytes 2000000 | tf_op jit(solution)/shard_map/pallas_call | solution.py:545
  51.6 1.5 %copy.8 = f32[64,2,128]{2,1,0:T(2,128)} copy(f32[64,2,128]{2,1,0:T(2,128)} %bitcast.6) | data formatting | bytes 131072
  53.1 1.6 %copy.9 = f32[3,64,2,128]{3,2,1,0:T(2,128)} copy(f32[3,64,2,128]{3,2,1,0:T(2,128)} %bitcast.5) | data formatting | bytes 393216

commit v5 on v4

--- a/solution.py
+++ b/solution.py
@@ -26,7 +26,7 @@
 SAME = 8
 UNITS = 10
 SAME_ROWS = 16
-JOINT_ROWS = 16
+JOINT_ROWS = 32
 JOINT_UNROLL = 16
 OUTER_ROWS = 32
 OUTER_UNROLL = 16

time: 54.9 us -> 54.6 us (level)
  no operation moved by 1% of the time
where the time goes in v5:
time: 54.6 us; the launch traced here: 54.4 us
  Pallas kernels  50.7 us (93%)
  local copies, waits for them, and re-layouts  3.09 us (6%)
  between operations  0.64 us (1%)
    pallas_call x1, Pallas kernels, on_device(): pl.pallas_call(functools.partial(kernel, gx_count, gy_count), out_shape=(...  50.7 us
    unnamed x2, local copies, waits for them, and re-layouts  3.09 us

profile of v5, /device:TPU:64, one launch (start us, length us, event | category | flops | bytes accessed | tf_op | source)
XLA Modules:
  0.0 54.4 jit_solution(6314491620216835411)
XLA Ops:
  0.6 50.7 %shard_map.59 = (f32[128,128]{1,0:T(8,128)}, f32[3,128,128]{2,1,0:T(8,128)}) custom-call(f32[3,128,128]{2,1,0:T(8,128)} %bitcast.7, f32[3,128,128]{2,1,0:T(8,128)} %bitcast.8, f32[128,128]{1,0:T(8,128)} %bitcast.9, s32[2,128]{1,0:T(2,128)} %counts_hbm.1), custom_call_target="tpu_custom_call" | custom-call | flops 400000000 | bytes 2000000 | tf_op jit(solution)/shard_map/pallas_call | solution.py:545
  51.3 1.5 %copy.8 = f32[64,2,128]{2,1,0:T(2,128)} copy(f32[64,2,128]{2,1,0:T(2,128)} %bitcast.6) | data formatting | bytes 131072
  52.8 1.6 %copy.9 = f32[3,64,2,128]{3,2,1,0:T(2,128)} copy(f32[3,64,2,128]{3,2,1,0:T(2,128)} %bitcast.5) | data formatting | bytes 393216
